TPU v7x, 32 devices: a whole 2x2x4 slice. The times are simulated.
32 devices in a mesh: blk: 16 (over z, y, x), mp: 2 (over core).
Axes of the slice: x: 2, y: 2, z: 4, core: 2. Of those that a mesh axis runs over, the one named last changes fastest.
Arguments:
- decoder_in: bfloat16 [8192, 768], P(('blk', 'mp')), may hold values from -6 to 6
- encoder_out: bfloat16 [2048, 768], P('blk'), may hold values from -6 to 6
- out_grad: bfloat16 [8192, 768], P(('blk', 'mp')), may hold values from -6 to 6
- block_items: int32 [32], P('blk'), may hold values from 0 to 15, as said below
- block_lengths: int32 [32], P('blk'), may hold values from 16 to 64
- target_lengths: int32 [16], P('blk'), may hold values from 128 to 512
- self_proj: float32 [3, 768, 768], P(None, 'blk', 'mp'), may hold values from -0.078125 to 0.078125
- self_out: float32 [768, 768], P('mp', 'blk'), may hold values from -1.25 to 1.25
- cross_proj: float32 [3, 768, 768], P(None, 'blk', 'mp'), may hold values from -0.078125 to 0.078125
- cross_out: float32 [768, 768], P('mp', 'blk'), may hold values from -3 to 3
- feed_in: float32 [2, 768, 2048], P(None, 'blk', 'mp'), may hold values from -0.21875 to 0.21875
- feed_out: float32 [2048, 768], P('mp', 'blk'), may hold values from -0.125 to 0.125
- norm_gains: float32 [3, 768], replicated, may hold values from 0.5 to 1.5
- position_bias: float32 [32, 12], replicated, may hold values from -3 to 3
- first_self_proj: float32 [3, 768, 768], P(None, 'blk', 'mp'), may hold values from -0.00021362305 to 0.00021362305
- first_self_out: float32 [768, 768], P('mp', 'blk'), may hold values from -2.2888184e-05 to 2.2888184e-05
- first_cross_proj: float32 [3, 768, 768], P(None, 'blk', 'mp'), may hold values from -0.00021362305 to 0.00021362305
- first_cross_out: float32 [768, 768], P('mp', 'blk'), may hold values from -1.1444092e-05 to 1.1444092e-05
- first_feed_in: float32 [2, 768, 2048], P(None, 'blk', 'mp'), may hold values from -4.5776367e-05 to 4.5776367e-05
- first_feed_out: float32 [2048, 768], P('mp', 'blk'), may hold values from -6.1035156e-05 to 6.1035156e-05
- first_gains: float32 [3, 768], replicated, may hold values from -0.00015258789 to 0.00015258789
- first_bias: float32 [32, 12], replicated, may hold values from -0.00010681152 to 0.00010681152
- second_self_proj: float32 [3, 768, 768], P(None, 'blk', 'mp'), may hold values from 1.0593364e-10 to 4.2373455e-10
- second_self_out: float32 [768, 768], P('mp', 'blk'), may hold values from 1.2712036e-12 to 5.0848145e-12
- second_cross_proj: float32 [3, 768, 768], P(None, 'blk', 'mp'), may hold values from 1.0593364e-10 to 4.2373455e-10
- second_cross_out: float32 [768, 768], P('mp', 'blk'), may hold values from 3.178009e-13 to 1.2712036e-12
- second_feed_in: float32 [2, 768, 2048], P(None, 'blk', 'mp'), may hold values from 4.2373457e-12 to 1.6949383e-11
- second_feed_out: float32 [2048, 768], P('mp', 'blk'), may hold values from 1.0593364e-11 to 4.2373455e-11
- second_gains: float32 [3, 768], replicated, may hold values from 5.296682e-11 to 2.1186727e-10
- second_bias: float32 [32, 12], replicated, may hold values from 2.4364738e-11 to 9.745895e-11
Outputs:
- layer_out: bfloat16 [8192, 768], P(('blk', 'mp'))
- decoder_grad: float32 [8192, 768], P(('blk', 'mp'))
- encoder_grad: float32 [2048, 768], P('blk', 'mp')
- new_self_proj: float32 [3, 768, 768], P(None, 'blk', 'mp')
- new_self_out: float32 [768, 768], P('mp', 'blk')
- new_cross_proj: float32 [3, 768, 768], P(None, 'blk', 'mp')
- new_cross_out: float32 [768, 768], P('mp', 'blk')
- new_feed_in: float32 [2, 768, 2048], P(None, 'blk', 'mp')
- new_feed_out: float32 [2048, 768], P('mp', 'blk')
- new_gains: float32 [3, 768], replicated
- new_bias: float32 [32, 12], replicated
- moment_self_proj: float32 [3, 768, 768], P(None, 'blk', 'mp')
- moment_self_out: float32 [768, 768], P('mp', 'blk')
- moment_cross_proj: float32 [3, 768, 768], P(None, 'blk', 'mp')
- moment_cross_out: float32 [768, 768], P('mp', 'blk')
- moment_feed_in: float32 [2, 768, 2048], P(None, 'blk', 'mp')
- moment_feed_out: float32 [2048, 768], P('mp', 'blk')
- moment_gains: float32 [3, 768], replicated
- moment_bias: float32 [32, 12], replicated
- square_self_proj: float32 [3, 768, 768], P(None, 'blk', 'mp')
- square_self_out: float32 [768, 768], P('mp', 'blk')
- square_cross_proj: float32 [3, 768, 768], P(None, 'blk', 'mp')
- square_cross_out: float32 [768, 768], P('mp', 'blk')
- square_feed_in: float32 [2, 768, 2048], P(None, 'blk', 'mp')
- square_feed_out: float32 [2048, 768], P('mp', 'blk')
- square_gains: float32 [3, 768], replicated
- square_bias: float32 [32, 12], replicated
- grad_norm: float32 [], replicated
- token_rms: float32 [2], replicated
Inputs may be any that keep to these rules, and one draw needn't show every extreme that they name: `block_items`: every one of the 16 items owns at least one block.
All inputs are finite; a program needn't handle non-finite values.
Results may differ from a plain program's by a relative error of at most 0.019.
Values may be sent and summed in bfloat16 or wider, within the bound.
A program may use at most 256 MiB of HBM per device.

v0:
```python
import math

import jax
import jax.numpy as jnp
import numpy as np
from jax import lax
from jax.sharding import PartitionSpec as P

D = 768
DH = 64
KB = 64
STEP = 10


norm_eps = 1e-06
clip_limit = 1.0
learn_rates = (0.02, 0.2, 0.02, 0.5, 0.02, 0.02, 1.0, 0.5)
beta_one = 0.9
beta_two = 0.999
adam_eps = 1e-08
weight_decay = 0.01
masked_score = -1000000000.0
key_block = 2048
HIGHEST = lax.Precision.HIGHEST
edge_table = np.ceil(16.0 * 8.0 ** (np.arange(16) / 16.0)).astype(np.int32)


def bucket_table(length):
    places = jnp.arange(length, dtype=jnp.int32)
    distance = jnp.maximum(places[:, None] - places[None, :], 0)
    edges = jnp.asarray(edge_table)
    above = jnp.sum((distance[:, :, None] >= edges[None, None, :]).astype(jnp.int32), axis=2)
    return jnp.where(distance < 16, distance, 15 + above)


def rms_norm(values, gain):
    return values * lax.rsqrt(jnp.mean(values * values, axis=-1, keepdims=True) + norm_eps) * gain


def norm_back(values, gain, upstream):
    scale = lax.rsqrt(jnp.mean(values * values, axis=-1, keepdims=True) + norm_eps)
    weighted = upstream * gain
    inner = jnp.mean(weighted * values, axis=-1, keepdims=True)
    return (
        scale * weighted - values * scale * scale * scale * inner,
        jnp.sum(upstream * values * scale, axis=0),
    )


def adamw(weight, moment, second, grad, decay, rate):
    moment = beta_one * moment + (1.0 - beta_one) * grad
    second = beta_two * second + (1.0 - beta_two) * grad * grad
    fixed_first = moment / (1.0 - beta_one**STEP)
    fixed_second = second / (1.0 - beta_two**STEP)
    weight = weight - rate * (fixed_first / (jnp.sqrt(fixed_second) + adam_eps) + decay * weight)
    return (weight, moment, second)


def to_heads(values):
    return lax.all_gather(values, "mp", axis=0, tiled=True)


def from_heads(terms):
    return lax.psum_scatter(terms, "mp", scatter_dimension=0, tiled=True)


def split_blocks(arrays, total):
    stride = math.gcd(total, key_block)
    return (
        tuple((member.reshape((total // stride, stride) + member.shape[1:]) for member in arrays)),
        stride,
    )


def cross_scores(queries, key_piece, tag_piece, query_items):
    heads_here = queries.shape[1]
    keys = key_piece.reshape(key_piece.shape[0], heads_here, DH)
    scores = jnp.einsum("qhd,khd->hqk", queries, keys, preferred_element_type=jnp.float32)
    return jnp.where(tag_piece[None, None, :] == query_items[None, :, None], scores, masked_score)


def attend_piece(state, piece, queries, query_items):
    heads_here = queries.shape[1]
    blocks, stride = split_blocks(piece, piece[0].shape[0])

    def inner(carried, block):
        running_max, totals, weighted = carried
        scores = cross_scores(queries, block[0], block[2], query_items)
        new_max = jnp.maximum(running_max, jnp.max(scores, axis=-1))
        factor = jnp.exp(running_max - new_max)
        weights_now = jnp.exp(scores - new_max[:, :, None])
        value_rows = block[1].reshape(stride, heads_here, DH).astype(jnp.float32)
        totals = totals * factor + jnp.sum(weights_now, axis=-1)
        weighted = weighted * factor[:, :, None] + jnp.einsum(
            "hqk,khd->hqd", weights_now, value_rows, precision=HIGHEST
        )
        return ((new_max, totals, weighted), None)

    state, _ = lax.scan(inner, state, blocks)
    return state


def body(
    decoder_in,
    encoder_out,
    out_grad,
    block_items,
    block_lengths,
    target_lengths,
    self_proj,
    self_out,
    cross_proj,
    cross_out,
    feed_in,
    feed_out,
    norm_gains,
    position_bias,
    first_self_proj,
    first_self_out,
    first_cross_proj,
    first_cross_out,
    first_feed_in,
    first_feed_out,
    first_gains,
    first_bias,
    second_self_proj,
    second_self_out,
    second_cross_proj,
    second_cross_out,
    second_feed_in,
    second_feed_out,
    second_gains,
    second_bias,
):
    head_rank = lax.axis_index("mp")
    cycle_rank = lax.axis_index("blk")
    local_rows = decoder_in.shape[0]
    group_rows = local_rows * lax.axis_size("mp")
    sequences = target_lengths.shape[0]
    length = group_rows // sequences
    half_width = self_proj.shape[2]
    heads_here = half_width // DH
    key_rows = encoder_out.shape[0]
    proj_self, out_self, proj_cross, out_cross, feed_up, feed_down = (
        lax.all_gather(self_proj.astype(jnp.bfloat16), "blk", axis=1, tiled=True),
        lax.all_gather(self_out.astype(jnp.bfloat16), "blk", axis=1, tiled=True),
        lax.all_gather(cross_proj.astype(jnp.bfloat16), "blk", axis=1, tiled=True),
        lax.all_gather(cross_out.astype(jnp.bfloat16), "blk", axis=1, tiled=True),
        lax.all_gather(feed_in.astype(jnp.bfloat16), "blk", axis=1, tiled=True),
        lax.all_gather(feed_out.astype(jnp.bfloat16), "blk", axis=1, tiled=True),
    )
    tokens = decoder_in.astype(jnp.float32)
    normed_one = rms_norm(tokens, norm_gains[0]).astype(jnp.bfloat16)
    wide_one = to_heads(normed_one)
    triple = jnp.einsum("rd,cde->cre", wide_one, proj_self, preferred_element_type=jnp.float32)
    shaped = triple.astype(jnp.bfloat16).reshape(3, sequences, length, heads_here, DH)
    queries, keys, values = (shaped[0], shaped[1], shaped[2])
    buckets = bucket_table(length)
    one_hot = (
        buckets[:, :, None] == jnp.arange(position_bias.shape[0], dtype=jnp.int32)[None, None, :]
    ).astype(jnp.float32)
    bias_here = lax.dynamic_slice_in_dim(position_bias, head_rank * heads_here, heads_here, 1)
    bias_full = jnp.einsum("qkb,bh->hqk", one_hot, bias_here, precision=HIGHEST)
    places = jnp.arange(length, dtype=jnp.int32)
    causal = places[:, None] >= places[None, :]
    scores = (
        jnp.einsum("sqhd,skhd->shqk", queries, keys, preferred_element_type=jnp.float32)
        + bias_full[None]
    )
    scores = jnp.where(causal[None, None], scores, masked_score)
    probs = jnp.exp(scores - jnp.max(scores, axis=-1, keepdims=True))
    probs = probs / jnp.sum(probs, axis=-1, keepdims=True)
    probs_low = probs.astype(jnp.bfloat16)
    attended = jnp.einsum("shqk,skhd->sqhd", probs_low, values, preferred_element_type=jnp.float32)
    attended = attended.astype(jnp.bfloat16).reshape(group_rows, half_width)
    after_one = tokens + from_heads(jnp.dot(attended, out_self, preferred_element_type=jnp.float32))
    normed_two = rms_norm(after_one, norm_gains[1]).astype(jnp.bfloat16)
    wide_two = to_heads(normed_two)
    cross_queries = jnp.dot(wide_two, proj_cross[0], preferred_element_type=jnp.float32)
    cross_queries = cross_queries.astype(jnp.bfloat16).reshape(group_rows, heads_here, DH)
    key_value = jnp.einsum(
        "ed,cdf->cef", encoder_out, proj_cross[1:], preferred_element_type=jnp.float32
    )
    key_value = key_value.astype(jnp.bfloat16)
    enc_keys, enc_values = (key_value[0], key_value[1])
    enc_places = jnp.arange(key_rows, dtype=jnp.int32)
    key_tags = jnp.where(
        enc_places % KB < jnp.repeat(block_lengths, KB), jnp.repeat(block_items, KB), -1
    )
    query_items = cycle_rank * sequences + jnp.arange(group_rows, dtype=jnp.int32) // length
    start_state = (
        jnp.full((heads_here, group_rows), masked_score, jnp.float32),
        jnp.zeros((heads_here, group_rows), jnp.float32),
        jnp.zeros((heads_here, group_rows, DH), jnp.float32),
    )
    state = attend_piece(
        start_state,
        (
            lax.all_gather(enc_keys, "blk", axis=0, tiled=True),
            lax.all_gather(enc_values, "blk", axis=0, tiled=True),
            lax.all_gather(key_tags, "blk", axis=0, tiled=True),
        ),
        cross_queries,
        query_items,
    )
    running_max, totals, weighted = state
    log_total = running_max + jnp.log(totals)
    cross_attended = jnp.transpose(weighted / totals[:, :, None], (1, 0, 2)).reshape(
        group_rows, half_width
    )
    cross_attended = cross_attended.astype(jnp.bfloat16)
    after_two = after_one + from_heads(
        jnp.dot(cross_attended, out_cross, preferred_element_type=jnp.float32)
    )
    normed_three = rms_norm(after_two, norm_gains[2]).astype(jnp.bfloat16)
    wide_three = to_heads(normed_three)
    gate_up = jnp.einsum("rd,cdf->crf", wide_three, feed_up, preferred_element_type=jnp.float32)

    def gated(gate, upper):
        return jax.nn.gelu(gate, approximate=True) * upper

    hidden_full, gated_pull = jax.vjp(gated, gate_up[0], gate_up[1])
    hidden = hidden_full.astype(jnp.bfloat16)
    layer_value = after_two + from_heads(
        jnp.dot(hidden, feed_down, preferred_element_type=jnp.float32)
    )
    row_index = head_rank * local_rows + jnp.arange(local_rows, dtype=jnp.int32)
    local_sequence = row_index // length
    sequence_limit = jnp.sum(
        jnp.where(
            local_sequence[:, None] == jnp.arange(sequences, dtype=jnp.int32)[None, :],
            target_lengths[None, :],
            0,
        ),
        axis=1,
    )
    valid = (row_index % length < sequence_limit).astype(jnp.float32)[:, None]
    upstream = out_grad.astype(jnp.float32) * valid
    wide_grad = to_heads(upstream.astype(jnp.bfloat16))
    grad_down = jnp.dot(hidden.T, wide_grad, preferred_element_type=jnp.float32)
    grad_gate, grad_upper = gated_pull(
        jnp.dot(wide_grad, feed_down.T, preferred_element_type=jnp.float32)
    )
    grad_pair = jnp.stack([grad_gate, grad_upper]).astype(jnp.bfloat16)
    grad_up = jnp.einsum("rd,crf->cdf", wide_three, grad_pair, preferred_element_type=jnp.float32)
    norm_three = from_heads(
        jnp.einsum("crf,cdf->rd", grad_pair, feed_up, preferred_element_type=jnp.float32)
    )
    delta_three, gain_three = norm_back(after_two, norm_gains[2], norm_three)
    grad_two = upstream + delta_three
    wide_grad = to_heads(grad_two.astype(jnp.bfloat16))
    grad_cout = jnp.dot(cross_attended.T, wide_grad, preferred_element_type=jnp.float32)
    grad_cross_out = jnp.dot(wide_grad, out_cross.T, preferred_element_type=jnp.float32)
    grad_cross_out = grad_cross_out.astype(jnp.bfloat16).reshape(group_rows, heads_here, DH)
    grad_out_full = grad_cross_out.astype(jnp.float32)
    gathered = (
        lax.all_gather(enc_keys, "blk", axis=0, tiled=True),
        lax.all_gather(enc_values, "blk", axis=0, tiled=True),
        lax.all_gather(key_tags, "blk", axis=0, tiled=True),
    )
    blocks, stride = split_blocks(gathered, gathered[0].shape[0])

    def rebuild(block):
        rows_here = block[0].shape[0]
        scores_here = cross_scores(cross_queries, block[0], block[2], query_items)
        probs_here = jnp.exp(scores_here - log_total[:, :, None])
        value_rows = block[1].reshape(rows_here, heads_here, DH)
        dprob = jnp.einsum(
            "qhd,khd->hqk", grad_cross_out, value_rows, preferred_element_type=jnp.float32
        )
        return (probs_here, dprob)

    def delta_step(running, block):
        probs_here, dprob = rebuild(block)
        return (running + jnp.sum(probs_here * dprob, axis=-1), None)

    delta_cross, _ = lax.scan(delta_step, jnp.zeros((heads_here, group_rows), jnp.float32), blocks)

    def query_step(running, block):
        probs_here, dprob = rebuild(block)
        dscore = (probs_here * (dprob - delta_cross[:, :, None])).astype(jnp.bfloat16)
        key_part = block[0].reshape(block[0].shape[0], heads_here, DH)
        return (
            running
            + jnp.einsum("hqk,khd->qhd", dscore, key_part, preferred_element_type=jnp.float32),
            None,
        )

    grad_query_full, _ = lax.scan(
        query_step, jnp.zeros((group_rows, heads_here, DH), jnp.float32), blocks
    )
    grad_query = grad_query_full.reshape(group_rows, half_width).astype(jnp.bfloat16)

    def key_terms():
        piece = tuple((member for member in gathered))
        parts, inner_stride = split_blocks(piece, key_rows * lax.axis_size("blk"))

        def key_step(block):
            probs_here, dprob = rebuild(block)
            dscore = (probs_here * (dprob - delta_cross[:, :, None])).astype(jnp.bfloat16)
            grad_keys = jnp.einsum(
                "hqk,qhd->khd", dscore, cross_queries, preferred_element_type=jnp.float32
            )
            grad_values = jnp.einsum("hqk,qhd->khd", probs_here, grad_out_full, precision=HIGHEST)
            return jnp.concatenate(
                [
                    grad_keys.reshape(inner_stride, half_width),
                    grad_values.reshape(inner_stride, half_width),
                ],
                axis=1,
            )

        return lax.map(key_step, parts).reshape(key_rows * lax.axis_size("blk"), 2 * half_width)

    key_grads = lax.psum_scatter(key_terms(), "blk", scatter_dimension=0, tiled=True).astype(
        jnp.bfloat16
    )
    grad_keys_low = key_grads[:, :half_width]
    grad_values_low = key_grads[:, half_width:]
    grad_ckey = jnp.dot(encoder_out.T, grad_keys_low, preferred_element_type=jnp.float32)
    grad_cvalue = jnp.dot(encoder_out.T, grad_values_low, preferred_element_type=jnp.float32)
    encoder_term = jnp.dot(
        grad_keys_low, proj_cross[1].T, preferred_element_type=jnp.float32
    ) + jnp.dot(grad_values_low, proj_cross[2].T, preferred_element_type=jnp.float32)
    encoder_grad = lax.psum_scatter(
        encoder_term.astype(jnp.bfloat16), "mp", scatter_dimension=1, tiled=True
    ).astype(jnp.float32)
    grad_cquery = jnp.dot(wide_two.T, grad_query, preferred_element_type=jnp.float32)
    norm_two = from_heads(jnp.dot(grad_query, proj_cross[0].T, preferred_element_type=jnp.float32))
    delta_two, gain_two = norm_back(after_one, norm_gains[1], norm_two)
    grad_one = grad_two + delta_two
    wide_grad = to_heads(grad_one.astype(jnp.bfloat16))
    grad_sout = jnp.dot(attended.T, wide_grad, preferred_element_type=jnp.float32)
    grad_attended = jnp.dot(wide_grad, out_self.T, preferred_element_type=jnp.float32)
    grad_attended = grad_attended.astype(jnp.bfloat16).reshape(sequences, length, heads_here, DH)
    dprob_self = jnp.einsum(
        "sqhd,skhd->shqk", grad_attended, values, preferred_element_type=jnp.float32
    )
    delta_self = jnp.sum(probs * dprob_self, axis=-1, keepdims=True)
    dscore_self = (probs * (dprob_self - delta_self)).astype(jnp.bfloat16)
    grad_bias_here = jnp.einsum(
        "hqk,qkb->bh", jnp.sum(dscore_self.astype(jnp.float32), axis=0), one_hot, precision=HIGHEST
    )
    grad_bias = lax.dynamic_update_slice_in_dim(
        jnp.zeros(position_bias.shape, jnp.float32), grad_bias_here, head_rank * heads_here, 1
    )
    grad_queries = jnp.einsum(
        "shqk,skhd->sqhd", dscore_self, keys, preferred_element_type=jnp.float32
    )
    grad_keys = jnp.einsum(
        "shqk,sqhd->skhd", dscore_self, queries, preferred_element_type=jnp.float32
    )
    grad_values = jnp.einsum(
        "shqk,sqhd->skhd", probs_low, grad_attended, preferred_element_type=jnp.float32
    )
    grad_triple = jnp.stack([grad_queries, grad_keys, grad_values]).astype(jnp.bfloat16)
    grad_triple = grad_triple.reshape(3, group_rows, half_width)
    grad_sproj = jnp.einsum(
        "rd,cre->cde", wide_one, grad_triple, preferred_element_type=jnp.float32
    )
    norm_one = from_heads(
        jnp.einsum("cre,cde->rd", grad_triple, proj_self, preferred_element_type=jnp.float32)
    )
    delta_one, gain_one = norm_back(tokens, norm_gains[0], norm_one)
    decoder_grad = grad_one + delta_one
    grad_cproj = jnp.stack([grad_cquery, grad_ckey, grad_cvalue])
    shards = (
        lax.psum_scatter(grad_sproj, "blk", scatter_dimension=1, tiled=True),
        lax.psum_scatter(grad_sout, "blk", scatter_dimension=1, tiled=True),
        lax.psum_scatter(grad_cproj, "blk", scatter_dimension=1, tiled=True),
        lax.psum_scatter(grad_cout, "blk", scatter_dimension=1, tiled=True),
        lax.psum_scatter(grad_up, "blk", scatter_dimension=1, tiled=True),
        lax.psum_scatter(grad_down, "blk", scatter_dimension=1, tiled=True),
    )
    square_sum = sum((jnp.sum(member * member) for member in shards))
    stat_terms = jnp.stack(
        [
            jnp.sum(valid * layer_value * layer_value),
            jnp.sum(valid * decoder_grad * decoder_grad),
            jnp.sum(valid),
        ]
    )
    gain_grads, bias_grads, square_total, stat_total = lax.psum(
        (jnp.stack([gain_one, gain_two, gain_three]), grad_bias, square_sum, stat_terms),
        ("blk", "mp"),
    )
    grad_norm = jnp.sqrt(
        square_total + jnp.sum(gain_grads * gain_grads) + jnp.sum(bias_grads * bias_grads)
    )
    factor = jnp.minimum(1.0, clip_limit / (grad_norm + 1e-06))
    params = (
        self_proj,
        self_out,
        cross_proj,
        cross_out,
        feed_in,
        feed_out,
        norm_gains,
        position_bias,
    )
    firsts = (
        first_self_proj,
        first_self_out,
        first_cross_proj,
        first_cross_out,
        first_feed_in,
        first_feed_out,
        first_gains,
        first_bias,
    )
    seconds = (
        second_self_proj,
        second_self_out,
        second_cross_proj,
        second_cross_out,
        second_feed_in,
        second_feed_out,
        second_gains,
        second_bias,
    )
    gradients = (
        shards[0],
        shards[1],
        shards[2],
        shards[3],
        shards[4],
        shards[5],
        gain_grads,
        bias_grads,
    )
    new_weights = []
    new_firsts = []
    new_seconds = []
    for index in range(8):
        decay = weight_decay if index < 6 else 0.0
        weight, moment, second = adamw(
            params[index],
            firsts[index],
            seconds[index],
            gradients[index] * factor,
            decay,
            learn_rates[index],
        )
        new_weights.append(weight)
        new_firsts.append(moment)
        new_seconds.append(second)
    token_rms = jnp.sqrt(stat_total[:2] / (stat_total[2] * D))
    return (
        layer_value.astype(jnp.bfloat16),
        decoder_grad,
        encoder_grad,
        new_weights[0],
        new_weights[1],
        new_weights[2],
        new_weights[3],
        new_weights[4],
        new_weights[5],
        new_weights[6],
        new_weights[7],
        new_firsts[0],
        new_firsts[1],
        new_firsts[2],
        new_firsts[3],
        new_firsts[4],
        new_firsts[5],
        new_firsts[6],
        new_firsts[7],
        new_seconds[0],
        new_seconds[1],
        new_seconds[2],
        new_seconds[3],
        new_seconds[4],
        new_seconds[5],
        new_seconds[6],
        new_seconds[7],
        grad_norm,
        token_rms,
    )


def solution(mesh):
    return jax.shard_map(
        body,
        mesh=mesh,
        in_specs=(
            P(("blk", "mp"), None),
            P("blk", None),
            P(("blk", "mp"), None),
            P("blk"),
            P("blk"),
            P("blk"),
            P(None, "blk", "mp"),
            P("mp", "blk"),
            P(None, "blk", "mp"),
            P("mp", "blk"),
            P(None, "blk", "mp"),
            P("mp", "blk"),
            P(),
            P(),
            P(None, "blk", "mp"),
            P("mp", "blk"),
            P(None, "blk", "mp"),
            P("mp", "blk"),
            P(None, "blk", "mp"),
            P("mp", "blk"),
            P(),
            P(),
            P(None, "blk", "mp"),
            P("mp", "blk"),
            P(None, "blk", "mp"),
            P("mp", "blk"),
            P(None, "blk", "mp"),
            P("mp", "blk"),
            P(),
            P(),
        ),
        out_specs=(
            P(("blk", "mp"), None),
            P(("blk", "mp"), None),
            P("blk", "mp"),
            P(None, "blk", "mp"),
            P("mp", "blk"),
            P(None, "blk", "mp"),
            P("mp", "blk"),
            P(None, "blk", "mp"),
            P("mp", "blk"),
            P(),
            P(),
            P(None, "blk", "mp"),
            P("mp", "blk"),
            P(None, "blk", "mp"),
            P("mp", "blk"),
            P(None, "blk", "mp"),
            P("mp", "blk"),
            P(),
            P(),
            P(None, "blk", "mp"),
            P("mp", "blk"),
            P(None, "blk", "mp"),
            P("mp", "blk"),
            P(None, "blk", "mp"),
            P("mp", "blk"),
            P(),
            P(),
            P(),
            P(),
        ),
        check_vma=False,
    )
```

profile of v0, /device:TPU:0, one launch (start us, length us, event | category | flops | bytes accessed | tf_op | source)
XLA Modules:
  0.0 1651.3 jit_solution(10308849454630375530)
XLA Ops:
  16.9 8.6 iota_compare_fusion
  25.5 46.3 %copy.177 = pred[512,512,32]{1,2,0:T(32,128)(4,1)} copy(pred[512,512,32]{0,2,1:T(32,128)(4,1)} %iota_compare_fusion) | data formatting | bytes 16777216 | tf_op jit(solution)/shard_map/eq | solution.py:160
  71.8 11.8 fusion.76
  83.7 9.2 copy.178
  95.8 47.5 %all_gather.50 = bf16[384,768]{0,1:T(8,128)(2,1)S(1)} all-gather(bf16[384,48]{0,1:T(8,128)(2,1)S(1)} %convert_element_type.149), channel_id=1, replica_groups=mesh['blk'=16,'mp'=2] {'blk'}, dimensions={1}, use_global_device_ids=true | all-gather | bytes 626688 | tf_op jit(solution)/shard_map/all_gather | solution.py:146
  163.9 35.3 %all-gather.2 = s32[16,1,128]{2,1,0:T(1,128)S(1)} all-gather(s32[1,1,128]{2,1,0:T(1,128)S(1)} %fusion.83), channel_id=1, replica_groups=mesh['blk'=16,'mp'=2] {'blk'}, dimensions={0}, use_global_device_ids=true | all-gather | bytes 8704 | tf_op jit(solution)/shard_map/all_gather | solution.py:201
  199.2 43.4 %all_gather.56 = bf16[384,768]{0,1:T(8,128)(2,1)S(1)} all-gather(bf16[384,48]{0,1:T(8,128)(2,1)S(1)} %convert_element_type.157), channel_id=1, replica_groups=mesh['blk'=16,'mp'=2] {'blk'}, dimensions={1}, use_global_device_ids=true | all-gather | bytes 626688 | tf_op jit(solution)/shard_map/all_gather | solution.py:148
  249.7 12.0 select_reduce_fusion
  261.7 11.7 fusion.1
  273.5 23.4 %all-gather.20.cloned.1.call-done = bf16[1,2048,384]{1,2,0:T(8,128)(2,1)} async-done(((bf16[1,128,384]{1,2,0:T(8,128)(2,1)}), bf16[1,2048,384]{1,2,0:T(8,128)(2,1)}) %all-gather.20.cloned.1.call-update) | async-done | bytes 1572880 | tf_op jit(solution)/shard_map/all_gather | solution.py:200
  296.9 21.8 %fusion.41 = bf16[512,6,64]{0,2,1:T(8,128)(2,1)S(1)} fusion(bf16[2048,6,64]{0,2,1:T(8,128)(2,1)} %bitcast.214, f32[6,512,2048]{2,1,0:T(8,128)} %get-tuple-element.304, f32[6,512]{1,0:T(8,128)S(1)} %broadcast_maximum_fusion, pred[512,2048]{1,0:T(8,128)(4,1)S(1)} %broadcast_compare_fusion, f32[512,6]{0,1:T(8,128)S(1)} %bitcast_add_fusion, ...), kind=kOutput, calls=%fused_computation.86 | convolution fusion | flops 4845010944 | bytes 28217344 | tf_op jit(solution)/shard_map/while/body/eval_jaxpr/hqk,khd->hqd/dot_general | solution.py:94
  332.7 68.7 %all-gather.14.cloned.1.call-done = bf16[2,768,1024]{2,1,0:T(8,128)(2,1)} async-done(((bf16[2,48,1024]{2,1,0:T(8,128)(2,1)}), bf16[2,768,1024]{2,1,0:T(8,128)(2,1)}) %all-gather.14.cloned.1.call-update) | async-done | bytes 3145744 | tf_op jit(solution)/shard_map/all_gather | solution.py:149
  407.3 53.8 %all-gather.16.cloned.1.call-done = bf16[1024,768]{0,1:T(8,128)(2,1)} async-done(((bf16[1024,48]{0,1:T(8,128)(2,1)}), bf16[1024,768]{0,1:T(8,128)(2,1)}) %all-gather.16.cloned.1.call-update) | async-done | bytes 1572880 | tf_op jit(solution)/shard_map/all_gather | solution.py:150
  461.2 6.4 fusion.39
  479.9 12.5 reduce-scatter.18.cloned.1.call-done
  502.1 17.4 %multiply_reduce_fusion = (f32[6,512]{1,0:T(8,128)S(1)}, f32[6,512,2048]{2,1,0:T(8,128)}) fusion(f32[6,512,2048]{2,1,0:T(8,128)} %get-tuple-element.304, f32[6,512]{1,0:T(8,128)S(1)} %get-tuple-element.299, pred[512,2048]{1,0:T(8,128)(4,1)S(1)} %broadcast_compare_fusion, bf16[512,6,64]{0,2,1:T(8,128)(2,1)S(1)} %bitcast.212, bf16[2048,6,64]{0,2,1:T(8,128)(2,1)} %bitcast.215), kind=kOutput, calls=%fused_computation.3 | convolution fusion | flops 830469120 | bytes 53370880 | tf_op jit(solution)/shard_map/while/body/eval_jaxpr/qhd,khd->hqk/dot_general | solution.py:268
  519.5 16.8 %multiply_convert_fusion = bf16[6,512,2048]{2,1,0:T(8,128)(2,1)S(1)} fusion(f32[6,512,2048]{2,1,0:T(8,128)} %get-tuple-element.306, f32[6,512,2048]{2,1,0:T(8,128)} %get-tuple-element.304, f32[6,512]{1,0:T(8,128)S(1)} %get-tuple-element.305, f32[6,512]{1,0:T(8,128)S(1)} %get-tuple-element.299, pred[512,2048]{1,0:T(8,128)(4,1)S(1)} %broadcast_compare_fusion), kind=kLoop, calls=%fused_computation.2 | loop fusion | flops 31457280 | bytes 63987712 | tf_op jit(solution)/shard_map/while/body/eval_jaxpr/convert_element_type | solution.py:281
  536.3 7.2 convolution_convert_fusion.1
  546.8 6.9 fusion.109
  553.7 19.1 %fusion.4 = f32[6,64,2048]{2,1,0:T(8,128)S(1)} fusion(bf16[512,6,64]{0,2,1:T(8,128)(2,1)S(1)} %bitcast.213, f32[6,512,2048]{2,1,0:T(8,128)} %get-tuple-element.304, f32[6,512]{1,0:T(8,128)S(1)} %get-tuple-element.299, pred[512,2048]{1,0:T(8,128)(4,1)S(1)} %broadcast_compare_fusion), kind=kOutput, calls=%fused_computation.11 | convolution fusion | flops 4844421120 | bytes 29765632 | tf_op jit(solution)/shard_map/while/body/eval_jaxpr/hqk,qhd->khd/dot_general | solution.py:304
  592.2 6.5 multiply_reduce_fusion.1
  598.7 6.5 fusion.30
  606.1 6.6 multiply_convert_fusion.1
  631.3 10.4 copy.193
  655.3 68.8 %reduce-scatter.26.cloned.1.call-done = f32[128,768]{0,1:T(8,128)} async-done(((f32[2048,768]{0,1:T(8,128)}), f32[128,768]{0,1:T(8,128)}) %reduce-scatter.26.cloned.1.call-update) | async-done | bytes 393232 | tf_op jit(solution)/shard_map/reduce_scatter | solution.py:315
  739.3 113.7 %reduce-scatter.30.cloned.1.call-done = f32[384,48]{0,1:T(8,128)} async-done(((f32[384,768]{0,1:T(8,128)}), f32[384,48]{0,1:T(8,128)}) %reduce-scatter.30.cloned.1.call-update) | async-done | bytes 73744 | tf_op jit(solution)/shard_map/reduce_scatter | solution.py:371
  854.6 7.2 fusion.35
  861.9 126.4 %reduce-scatter.32.cloned.1.call-done = f32[1024,48]{0,1:T(8,128)} async-done(((f32[1024,768]{0,1:T(8,128)}), f32[1024,48]{0,1:T(8,128)}) %reduce-scatter.32.cloned.1.call-update) | async-done | bytes 196624 | tf_op jit(solution)/shard_map/reduce_scatter | solution.py:373
  989.9 127.5 %reduce-scatter.28.cloned.1.call-done = f32[384,48]{0,1:T(8,128)} async-done(((f32[384,768]{0,1:T(8,128)}), f32[384,48]{0,1:T(8,128)}) %reduce-scatter.28.cloned.1.call-update) | async-done | bytes 73744 | tf_op jit(solution)/shard_map/reduce_scatter | solution.py:369
  1118.8 8.8 reduce-scatter.24.cloned.1.call-done
  1140.1 438.8 %all-reduce.7.cloned.1.call-done = (f32[3,768,384]{2,0,1:T(4,128)}, f32[3,768,384]{2,0,1:T(4,128)}, f32[2,768,1024]{2,0,1:T(2,128)}) async-done(((f32[3,768,384]{2,0,1:T(4,128)}, f32[3,768,384]{2,0,1:T(4,128)}, f32[2,768,1024]{2,0,1:T(2,128)}), (f32[3,768,384]{2,0,1:T(4,128)}, f32[3,768,384]{2,0,1:T(4,128)}, f32[2,768,1024]{2,0,1:T(2,128)})) %all-reduce.7.cloned.1.call-update) | async-done | bytes 13369360
  1587.4 40.0 %all-reduce.3 = (f32[]{:T(128)}, f32[3,768]{1,0:T(4,128)S(1)}, f32[32,12]{0,1:T(8,128)S(1)}, f32[3]{0:T(128)S(1)}) all-reduce(f32[]{:T(128)S(6)} %add.364, f32[3,768]{1,0:T(4,128)S(1)} %pad_maximum_fusion.8, f32[32,12]{0,1:T(8,128)S(1)} %dynamic_update_slice.6, ...), channel_id=1, replica_groups=mesh['blk'=16,'mp'=2] {'blk','mp'}, use_global_device_ids=true, to_apply=%region_33.34 | all-reduce | flops 2692 | bytes 21536 | tf_op jit(solution)/shard_map/psum | solution.py:383
  (294 shorter events, 185.6 us)
Async XLA Ops:
  7.2 153.8 %copy-start = (bf16[128,768]{1,0:T(8,128)(2,1)S(1)}, bf16[128,768]{1,0:T(8,128)(2,1)}, u32[]{:S(2)}) copy-start(bf16[128,768]{1,0:T(8,128)(2,1)} %param.32) | copy-start | bytes 589828
  7.2 136.0 %all-gather.10.cloned.1.call-start = ((), (), s32[]{:S(2)}) async-start(), calls=%async_computation.11 | async-start | bytes 1880064 | tf_op jit(solution)/shard_map/all_gather | solution.py:145
  8.9 152.0 %all-gather.12.cloned.1.call-start = ((), (), s32[]{:S(2)}) async-start(), calls=%async_computation.13 | async-start | bytes 1880064 | tf_op jit(solution)/shard_map/all_gather | solution.py:147
  10.6 232.7 %reduce-scatter.14.cloned.1.call-start = ((), (), s32[]{:S(2)}) async-start(), calls=%async_computation.12 | async-start | bytes 2359296 | tf_op jit(solution)/shard_map/reduce_scatter | solution.py:64
  160.9 88.8 %all-gather.18.cloned.1.call-start = ((), (), s32[]{:S(2)}) async-start(), calls=%async_computation.25 | async-start | bytes 1671168 | tf_op jit(solution)/shard_map/all_gather | solution.py:199
  163.5 133.5 %all-gather.20.cloned.1.call-start = ((), (), s32[]{:S(2)}) async-start(), calls=%async_computation.26 | async-start | bytes 1671168 | tf_op jit(solution)/shard_map/all_gather | solution.py:200
  243.2 85.5 %reduce-scatter.16.cloned.1.call-start = ((), (), s32[]{:S(2)}) async-start(), calls=%async_computation.14 | async-start | bytes 2359296 | tf_op jit(solution)/shard_map/reduce_scatter | solution.py:64
  321.4 80.0 %all-gather.14.cloned.1.call-start = ((), (), s32[]{:S(2)}) async-start(), calls=%async_computation.15 | async-start | bytes 3342336 | tf_op jit(solution)/shard_map/all_gather | solution.py:149
  322.2 139.0 %all-gather.16.cloned.1.call-start = ((), (), s32[]{:S(2)}) async-start(), calls=%async_computation.16 | async-start | bytes 1671168 | tf_op jit(solution)/shard_map/all_gather | solution.py:150
  323.8 156.1 %reduce-scatter.20.cloned.1.call-start = ((), (), s32[]{:S(2)}) async-start(), calls=%async_computation.18 | async-start | bytes 2359296 | tf_op jit(solution)/shard_map/reduce_scatter | solution.py:64
  472.0 20.4 %reduce-scatter.18.cloned.1.call-start = ((), (), s32[]{:S(2)}) async-start(), calls=%async_computation.17 | async-start | bytes 2359296 | tf_op jit(solution)/shard_map/reduce_scatter | solution.py:64
  476.0 107.3 %reduce-scatter.22.cloned.1.call-start = ((), (), s32[]{:S(2)}) async-start(), calls=%async_computation.19 | async-start | bytes 2359296 | tf_op jit(solution)/shard_map/reduce_scatter | solution.py:64
  546.6 177.5 %reduce-scatter.26.cloned.1.call-start = ((), (), s32[]{:S(2)}) async-start(), calls=%async_computation.21 | async-start | bytes 6684672 | tf_op jit(solution)/shard_map/reduce_scatter | solution.py:315
  576.3 276.8 %reduce-scatter.30.cloned.1.call-start = ((), (), s32[]{:S(2)}) async-start(), calls=%async_computation.23 | async-start | bytes 1253376 | tf_op jit(solution)/shard_map/reduce_scatter | solution.py:371
  579.2 409.1 %reduce-scatter.32.cloned.1.call-start = ((), (), s32[]{:S(2)}) async-start(), calls=%async_computation.24 | async-start | bytes 3342336 | tf_op jit(solution)/shard_map/reduce_scatter | solution.py:373
  583.2 534.1 %reduce-scatter.28.cloned.1.call-start = ((), (), s32[]{:S(2)}) async-start(), calls=%async_computation.22 | async-start | bytes 1253376 | tf_op jit(solution)/shard_map/reduce_scatter | solution.py:369
  591.9 535.7 %reduce-scatter.24.cloned.1.call-start = ((), (), s32[]{:S(2)}) async-start(), calls=%async_computation.20 | async-start | bytes 2359296 | tf_op jit(solution)/shard_map/reduce_scatter | solution.py:64
  625.0 514.0 %reduce-scatter.34.cloned.1.call-start = ((), (), s32[]{:S(2)}) async-start(), calls=%async_computation.27 | async-start | bytes 294912
  730.4 848.5 %all-reduce.7.cloned.1.call-start = ((), (), s32[]{:S(2)}) async-start(), calls=%async_computation.28 | async-start | bytes 31457280
  854.6 273.0 %copy-start.51 = (f32[768]{0:T(1024)S(1)}, f32[768]{0:T(1024)}, u32[]{:S(2)}) copy-start(f32[768]{0:T(1024)} %copy-done.50) | copy-start | bytes 9220
  854.6 273.0 %copy-start.59 = (f32[256]{0:T(256)S(1)}, f32[256]{0:T(256)}, u32[]{:S(2)}) copy-start(f32[256]{0:T(256)} %copy-done.58) | copy-start | bytes 3076
  861.8 770.7 %copy-start.55 = (f32[3,768]{1,0:T(4,128)S(1)}, f32[3,768]{1,0:T(4,128)}, u32[]{:S(2)}) copy-start(f32[3,768]{1,0:T(4,128)} %param.43) | copy-start | bytes 27652
  861.8 772.0 %copy-start.57 = (f32[32,12]{0,1:T(8,128)S(1)}, f32[32,12]{0,1:T(8,128)}, u32[]{:S(2)}) copy-start(f32[32,12]{0,1:T(8,128)} %param.44) | copy-start | bytes 4612
  861.8 773.5 %copy-start.28 = (f32[3,48,384]{2,1,0:T(8,128)S(1)}, f32[3,48,384]{2,1,0:T(8,128)}, u32[]{:S(2)}) copy-start(f32[3,48,384]{2,1,0:T(8,128)} %param.37) | copy-start | bytes 663556
  861.8 773.5 %copy-start.43 = (f32[3,48,384]{2,1,0:T(8,128)S(1)}, f32[3,48,384]{2,1,0:T(8,128)}, u32[]{:S(2)}) copy-start(f32[3,48,384]{2,1,0:T(8,128)} %param.45) | copy-start | bytes 663556
  1129.1 508.0 %copy-start.29 = (f32[3,48,384]{2,1,0:T(8,128)S(1)}, f32[3,48,384]{2,1,0:T(8,128)}, u32[]{:S(2)}) copy-start(f32[3,48,384]{2,1,0:T(8,128)} %param.39) | copy-start | bytes 663556
  1132.5 506.6 %copy-start.27 = (f32[2,48,1024]{2,1,0:T(8,128)S(1)}, f32[2,48,1024]{2,1,0:T(8,128)}, u32[]{:S(2)}) copy-start(f32[2,48,1024]{2,1,0:T(8,128)} %param.41) | copy-start | bytes 1179652
  1132.5 506.6 %copy-start.35 = (f32[2,48,1024]{2,1,0:T(8,128)S(1)}, f32[2,48,1024]{2,1,0:T(8,128)}, u32[]{:S(2)}) copy-start(f32[2,48,1024]{2,1,0:T(8,128)} %param.49) | copy-start | bytes 1179652
  1132.5 506.6 %copy-start.36 = (f32[2,48,1024]{2,1,0:T(8,128)S(1)}, f32[2,48,1024]{2,1,0:T(8,128)}, u32[]{:S(2)}) copy-start(f32[2,48,1024]{2,1,0:T(8,128)} %param.57) | copy-start | bytes 1179652
  1582.8 57.7 %copy-start.46 = (f32[384,48]{0,1:T(8,128)S(1)}, f32[384,48]{0,1:T(8,128)}, u32[]{:S(2)}) copy-start(f32[384,48]{0,1:T(8,128)} %param.46) | copy-start | bytes 221188
  1582.8 58.4 %copy-start.40 = (f32[384,48]{0,1:T(8,128)S(1)}, f32[384,48]{0,1:T(8,128)}, u32[]{:S(2)}) copy-start(f32[384,48]{0,1:T(8,128)} %param.40) | copy-start | bytes 221188
  1582.8 58.4 %copy-start.41 = (f32[384,48]{0,1:T(8,128)S(1)}, f32[384,48]{0,1:T(8,128)}, u32[]{:S(2)}) copy-start(f32[384,48]{0,1:T(8,128)} %reduce-scatter.30.cloned.1.call-done) | copy-start | bytes 221188
  (54 other events, 639.4 us)
Sparse Core Ops, SparseCore 0:
  11.3 61.6 all-gather.9
  76.3 60.1 all-gather.11
  161.0 4.9 reduce-scatter.13
  169.4 62.6 all-gather.17
  243.4 53.5 all-gather.19
  321.5 7.2 reduce-scatter.15
  332.0 69.3 all-gather.13
  404.8 56.3 all-gather.15
  472.1 7.7 reduce-scatter.19
  482.1 10.2 reduce-scatter.17
  546.7 10.2 reduce-scatter.21
  576.4 147.6 reduce-scatter.25
  729.6 123.4 reduce-scatter.29
  858.7 129.5 reduce-scatter.31
  993.6 123.6 reduce-scatter.27
  1119.5 8.0 reduce-scatter.23
  1130.2 8.7 reduce-scatter.33
  1145.3 433.5 all-reduce.6
where the time goes:
time: 1660 us; the launch traced here: 1650 us
  waiting for transfers between devices  1050 us (63%)
  matrix products  190 us (11%)
  blocking collectives  181 us (11%)
  other arithmetic  106 us (6%)
  local copies, waits for them, and re-layouts  94.7 us (6%)
  between operations  24.7 us (1%)
    unnamed x20, waiting for transfers between devices  444 us
    reduce_scatter x1, waiting for transfers between devices, body(): lax.psum_scatter(grad_sout, 'blk', scatter_dimension=1, tiled=True)  127 us
    reduce_scatter x1, waiting for transfers between devices, body(): lax.psum_scatter(grad_down, 'blk', scatter_dimension=1, tiled=True)  126 us
    reduce_scatter x1, waiting for transfers between devices, body(): lax.psum_scatter(grad_cout, 'blk', scatter_dimension=1, tiled=True)  114 us
    reduce_scatter x1, waiting for transfers between devices, body(): lax.psum_scatter(key_terms(), 'blk', scatter_dimension=0, tiled=True)  68.8 us
    all_gather x1, waiting for transfers between devices, body(): lax.all_gather(feed_in.astype(jnp.bfloat16), 'blk', axis=1, tiled=True)  68.7 us
    all_gather x1, waiting for transfers between devices, body(): lax.all_gather(feed_out.astype(jnp.bfloat16), 'blk', axis=1, tiled=True)  53.8 us
    all_gather x1, blocking collectives, body(): lax.all_gather(self_out.astype(jnp.bfloat16), 'blk', axis=1, tiled=True)  47.5 us
  transfers between devices with their start and end apart: 18, of which 13 were waited for; matrix products, arithmetic and copies ran while one was open for 17% of the time, Pallas kernels for 0%

commit v1 on v0

v1 whole, which is shorter than its diff:
```python
import functools
import math

import jax
import jax.numpy as jnp
import numpy as np
from jax import lax
from jax.experimental import pallas as pl
from jax.experimental.pallas import tpu as pltpu
from jax.sharding import PartitionSpec as P

D = 768
DH = 64
KB = 64
STEP = 10
MESH = pl.DeviceIdType.MESH
ANY = pl.BlockSpec(memory_space=pl.ANY)
VMEM = pl.BlockSpec(memory_space=pltpu.VMEM)

norm_eps = 1e-06
clip_limit = 1.0
learn_rates = (0.02, 0.2, 0.02, 0.5, 0.02, 0.02, 1.0, 0.5)
beta_one = 0.9
beta_two = 0.999
adam_eps = 1e-08
weight_decay = 0.01
masked_score = -1000000000.0
HIGHEST = lax.Precision.HIGHEST
BF = jnp.bfloat16
F32 = jnp.float32
edge_table = np.ceil(16.0 * 8.0 ** (np.arange(16) / 16.0)).astype(np.int32)


def bucket_of(distance):
    above = np.sum(distance[..., None] >= edge_table, axis=-1)
    return np.where(distance < 16, distance, 15 + above)


def rms_norm(values, gain):
    return values * lax.rsqrt(jnp.mean(values * values, axis=-1, keepdims=True) + norm_eps) * gain


def norm_back(values, gain, upstream):
    scale = lax.rsqrt(jnp.mean(values * values, axis=-1, keepdims=True) + norm_eps)
    weighted = upstream * gain
    inner = jnp.mean(weighted * values, axis=-1, keepdims=True)
    return (
        scale * weighted - values * scale * scale * scale * inner,
        jnp.sum(upstream * values * scale, axis=0),
    )


def adamw(weight, moment, second, grad, decay, rate):
    moment = beta_one * moment + (1.0 - beta_one) * grad
    second = beta_two * second + (1.0 - beta_two) * grad * grad
    fixed_first = moment / (1.0 - beta_one**STEP)
    fixed_second = second / (1.0 - beta_two**STEP)
    weight = weight - rate * (fixed_first / (jnp.sqrt(fixed_second) + adam_eps) + decay * weight)
    return (weight, moment, second)


def toeplitz_kernel(strip_ref, out_ref):
    @pl.loop(0, strip_ref.shape[0])
    def _(index):
        rows = jnp.broadcast_to(strip_ref[index], (128, 256))
        out_ref[index] = pltpu.roll(rows, 0, 1, stride=1, stride_axis=0)[:, :128]


class Place:
    def __init__(self, levels):
        self.levels = levels
        self.long = 2**levels
        self.me = lax.axis_index("blk")
        self.core = lax.axis_index("mp")
        self.p = lax.rem(self.me, 4)
        self.a = self.me // 4
        x = lax.rem(self.p, 2)
        y = self.p // 2
        dx = 1 - 2 * x
        dy = 2 - 4 * y
        d_first = dx + self.core * (dy - dx)
        d_second = dy + self.core * (dx - dy)
        self.p_first = self.p + d_first
        self.p_second = self.p + d_second
        self.p_both = self.p + dx + dy
        self.first = {"blk": self.me + d_first}
        self.second = {"blk": self.me + d_second}
        self.sibling = {"mp": 1 - self.core}
        self.in_plane = 2 * self.p + self.core

    def group(self, level):
        return (self.a // 2**level) * 2**level

    def other_group(self, level):
        bit = lax.rem(self.a // 2**level, 2)
        return self.group(level) + (1 - 2 * bit) * 2**level

    def partner(self, level):
        bit = lax.rem(self.a // 2**level, 2)
        return {"blk": self.me + (1 - 2 * bit) * 2**level * 4}

    def partners(self):
        near = [self.partner(level) for level in range(self.levels)]
        return near + [self.first, self.second, self.sibling]

    def plane_mate(self, step):
        other = lax.rem(self.in_plane + step, 8)
        return {"blk": self.me - self.p + other // 2, "mp": lax.rem(other, 2)}

    def line_mate(self, step):
        return {"blk": self.me + 4 * (lax.rem(self.a + step, self.long) - self.a)}

    def mates(self):
        return [self.plane_mate(step) for step in range(1, 8)] + [
            self.line_mate(step) for step in range(1, self.long)
        ]


def enter(partners):
    barrier = pltpu.get_barrier_semaphore()
    for device in partners:
        pl.semaphore_signal(barrier, inc=1, device_id=device, device_id_type=MESH)
    pl.semaphore_wait(barrier, len(partners))


class Copies:
    def __init__(self, send, recv):
        self.send, self.recv, self.count, self.open = send, recv, 0, []

    def remote(self, src, dst, device):
        index = self.count
        self.count += 1
        copy = pltpu.make_async_remote_copy(
            src_ref=src,
            dst_ref=dst,
            send_sem=self.send.at[index],
            recv_sem=self.recv.at[index],
            device_id=device,
            device_id_type=MESH,
        )
        copy.start()
        self.open.append(copy)
        return copy

    def left(self, copy):
        copy.wait_send()
        self.open = [member for member in self.open if member is not copy]

    def finish(self):
        for copy in self.open:
            copy.wait_send()
        self.open = []


class Moves:
    def __init__(self, semaphores):
        self.semaphores, self.count, self.open = semaphores, 0, {}

    def start(self, name, src, dst):
        copy = pltpu.make_async_copy(src, dst, self.semaphores.at[self.count])
        self.count += 1
        copy.start()
        self.open[name] = copy

    def need(self, *names):
        for name in names:
            if name in self.open:
                self.open.pop(name).wait()

    def finish(self):
        self.need(*list(self.open))


def dot(left, right, dims=((1,), (0,))):
    return lax.dot_general(left, right, (dims, ((), ())), preferred_element_type=F32)


NN = ((1,), (0,))
NT = ((1,), (1,))


LINK_BYTES = 1e5
DELAY = 1.5
BACKLOG = 2.0


class Pump:
    def __init__(self, gate, ahead):
        self.now = 0.0
        self.free = {}
        self.flying = []
        self.count = 0
        self.pending = []
        self.gate, self.ahead = gate, ahead

    def _resume(self, chain):
        try:
            loads, after = next(chain)
        except StopIteration:
            return
        for link, size in loads.items():
            self.free[link] = max(self.free.get(link, 0.0), self.now) + size / LINK_BYTES
        self.count += 1
        end = max(self.free[link] for link in loads)
        self.flying.append((end + DELAY, self.count, chain, after))

    def _ready(self, entry):
        return max(entry[0], self.free.get(entry[3], 0.0) - BACKLOG)

    def _start(self):
        while self.pending and self.free.get(self.gate, 0.0) <= self.now + self.ahead:
            self._resume(self.pending.pop(0))

    def _next(self):
        soonest = min(self.flying, key=lambda entry: (self._ready(entry), entry[1]))
        self.flying = [entry for entry in self.flying if entry is not soonest]
        self.now = max(self.now, self._ready(soonest))
        self._resume(soonest[2])
        self._start()

    def add(self, *chains):
        self.pending.extend(chains)
        self._start()

    def work(self, spent):
        end = self.now + spent
        while self.flying and min(self._ready(entry) for entry in self.flying) <= end:
            self._next()
        self.now = max(self.now, end)
        self._start()

    def until(self, chain):
        busy = lambda: any(entry[2] is chain for entry in self.flying)
        while busy() or any(member is chain for member in self.pending):
            if not self.flying:
                self.now = max(self.now, self.free.get(self.gate, 0.0) - self.ahead)
                self._start()
            else:
                self._next()

    def drain(self):
        while self.flying or self.pending:
            if not self.flying:
                self.now = max(self.now, self.free.get(self.gate, 0.0) - self.ahead)
                self._start()
            else:
                self._next()


def bytes_of(ref):
    size = 2 if ref.dtype == BF else 4
    return size * int(np.prod(ref.shape))


EVERY = slice(None)


class View:
    def __init__(self, ref, *lead, columns=slice(None)):
        self.ref, self.lead, self.columns = ref, lead, columns

    def _index(self, index):
        index = self.lead + index
        return index + (EVERY,) * (len(self.ref.shape) - 1 - len(index)) + (self.columns,)

    def at(self, *index):
        return self.ref.at[self._index(index)]

    def get(self, *index):
        return self.ref[self._index(index)]

    def put(self, value, *index):
        self.ref[self._index(index)] = value.astype(self.ref.dtype)


def line_load(level, size):
    return {"ends": size} if level == 0 else {"ends": 2**level * size, "middle": 4**level * size}


def gather_chain(place, copies, slot, plane_first=False):
    unit = 2.0 * bytes_of(slot(0, 0))

    def plane(a, weight, after):
        one = copies.remote(slot(a, place.p), slot(a, place.p), place.first)
        two = copies.remote(slot(a, place.p), slot(a, place.p), place.second)
        yield {"xy": unit * weight}, "xy"
        two.wait_recv()
        three = copies.remote(slot(a, place.p_second), slot(a, place.p_second), place.first)
        yield {"xy": unit * weight / 2}, after
        one.wait_recv()
        three.wait_recv()

    def line(p, weight, after):
        for level in range(place.levels):
            zs = place.a if level == 0 else pl.ds(place.group(level), 2**level)
            sent = copies.remote(slot(zs, p), slot(zs, p), place.partner(level))
            yield line_load(level, unit * weight), "middle" if level + 1 < place.levels else after
            sent.wait_recv()

    if plane_first:
        yield from plane(place.a, 1, "ends")
        yield from line(EVERY, 4, None)
    else:
        yield from line(place.p, 1, "xy")
        yield from plane(EVERY, place.long, None)


def add_up(*terms):
    total = terms[0].astype(F32)
    for term in terms[1:]:
        total = total + term.astype(F32)
    return total


def scatter_chain(place, copies, grads, two, one, total, zs, out):
    long = place.long
    unit = 2.0 * bytes_of(grads.at(0, 0))
    far = copies.remote(grads.at(EVERY, place.p_both), two.at(1), place.first)
    near = copies.remote(grads.at(EVERY, place.p_first), two.at(0), place.first)
    yield {"xy": unit * long}, "xy"
    far.wait_recv()

    for z in range(long):
        total.put(add_up(grads.get(z, place.p_second), two.get(1, z)), z)

    last = copies.remote(total.at(), one.at(), place.second)
    yield {"xy": unit * long / 2}, "middle"
    near.wait_recv()
    last.wait_recv()
    copies.left(last)
    sent = []

    for z in range(long):
        total.put(add_up(grads.get(z, place.p), two.get(0, z), one.get(z)), z)

    for level in reversed(range(place.levels)):
        away = pl.ds(place.other_group(level), 2**level)
        landing = pl.ds(2**level - 1, 2**level)
        copy = copies.remote(total.at(away), zs.at(landing), place.partner(level))
        sent.append(copy)
        yield line_load(level, unit), "ends" if level > 0 else None
        copy.wait_recv()
        if level == 0:
            out.put(add_up(total.get(place.a), zs.get(0)))
        else:
            for z in range(2**level):
                mine = place.group(level) + z
                total.put(add_up(total.get(mine), zs.get(2**level - 1 + z)), mine)
    for copy in sent:
        copies.left(copy)


def scatter_line_first(place, copies, grads, two, one, total, zs, out):
    unit = 2.0 * bytes_of(grads.at(0, 0))
    top = place.levels - 1
    local = lambda z: lax.rem(z, 2**top)
    for level in reversed(range(place.levels)):
        source, at = (grads, lambda z: z) if level == top else (total, local)
        away = pl.ds(at(place.other_group(level)), 2**level)
        landing = pl.ds(2**level - 1, 2**level)
        copy = copies.remote(source.at(away), zs.at(landing), place.partner(level))
        yield line_load(level, 4 * unit), "ends" if level > 0 else "xy"
        copy.wait_recv()

        for z in range(2**level):
            mine = place.group(level) + z
            for p in range(4):
                total.put(
                    add_up(source.get(at(mine), p), zs.get(2**level - 1 + z, p)), local(mine), p
                )

    here = local(place.a)
    far = copies.remote(total.at(here, place.p_both), two.at(1), place.first)
    near = copies.remote(total.at(here, place.p_first), two.at(0), place.first)
    yield {"xy": unit}, "xy"
    far.wait_recv()
    total.put(add_up(total.get(here, place.p_second), two.get(1)), here, place.p_second)
    last = copies.remote(total.at(here, place.p_second), one.at(), place.second)
    yield {"xy": unit / 2}, None
    near.wait_recv()
    last.wait_recv()
    out.put(add_up(total.get(here, place.p), two.get(0), one.get()))


def sum_chain(place, copies, mine, plane, middle, line, out):
    plane[place.in_plane] = mine[...]
    sent = [
        copies.remote(mine, plane.at[place.in_plane], place.plane_mate(step)) for step in range(1, 8)
    ]
    yield {"xy": 0.0}, "middle"
    for copy in sent:
        copy.wait_recv()
    total = plane[0]
    for index in range(1, 8):
        total = total + plane[index]
    middle[...] = total
    line[place.a] = total
    sent = [
        copies.remote(middle, line.at[place.a], place.line_mate(step))
        for step in range(1, place.long)
    ]
    yield {"middle": 0.0}, None
    for copy in sent:
        copy.wait_recv()
    total = line[0]
    for index in range(1, place.long):
        total = total + line[index]
    out[...] = total


def norm_rows(values, gain):
    return values * lax.rsqrt(jnp.mean(values * values, axis=-1, keepdims=True) + norm_eps) * gain


def head_mask(which):
    lane = lax.broadcasted_iota(jnp.int32, (1, 128), 1)
    return jnp.where(lane // DH == which, 1.0, 0.0).astype(BF)


def make_eye(eye):
    row = lax.broadcasted_iota(jnp.int32, eye.shape, 0)
    column = lax.broadcasted_iota(jnp.int32, eye.shape, 1)
    eye[...] = jnp.where(row == column, 1.0, 0.0).astype(BF)


def turn(value, eye):
    parts = []
    for start in range(0, value.shape[1], 256):
        size = min(256, value.shape[1] - start)
        piece = value[:, start : start + size]
        parts.append(dot(eye[pl.ds(0, size), pl.ds(0, size)], piece, NT).astype(BF))
    return parts[0] if len(parts) == 1 else jnp.concatenate(parts, axis=0)


def lanes_at(start, pair):
    return pl.ds(start + pair * 128, 128)


CHUNK = 64


def bias_rows(bias, head, tiles, tile, key):
    blank = jnp.full((128, 128), masked_score, F32)
    away = [2 * tile - key, 2 * tile + 1 - key]
    return jnp.concatenate(
        [bias[head * tiles + each] if each >= 0 else blank for each in away], axis=1
    )


def grouped(chunk):
    return chunk.reshape(chunk.shape[0] // 8, 8, chunk.shape[1])


def eight_rows(row):
    return jnp.broadcast_to(row, (8, row.shape[1]))[None]


def softmax_chunks(load, chunks, low_out):
    top = None
    for index in range(chunks):
        most = jnp.max(grouped(load(index)), axis=0)
        top = most if top is None else jnp.maximum(top, most)
    top = jnp.max(top, axis=0, keepdims=True)
    wide_top = eight_rows(top)
    total = None
    for index in range(chunks):
        shifted = jnp.exp(grouped(load(index)) - wide_top)
        part = jnp.sum(shifted, axis=0)
        total = part if total is None else total + part
        low_out(index, shifted.reshape(CHUNK, shifted.shape[2]).astype(BF))
    total = jnp.sum(total, axis=0, keepdims=True)
    return (total, top + jnp.log(total))


def back_chunk(scores, dprobs, log_total, inner):
    probs = jnp.exp(grouped(scores) - log_total)
    dscores = probs * (grouped(dprobs) - inner)
    return (probs.reshape(scores.shape).astype(BF), dscores.reshape(scores.shape).astype(BF))


def self_forward(pair, qkv, bias, o1, o1_turned, lse, eye, scores, low_probs, between):
    width = o1.shape[1]
    tiles = qkv.shape[0] // 128
    values_turned = turn(qkv[:, lanes_at(2 * width, pair)], eye)
    for tile in range(tiles // 2):
        rows, seen = pl.ds(tile * 256, 256), (tile + 1) * 256
        query = qkv[rows, lanes_at(0, pair)]
        key = qkv[pl.ds(0, seen), lanes_at(width, pair)]
        made = []
        for which in range(2):
            head = 2 * pair + which
            scores[which, pl.ds(0, seen), :] = dot(key, query * head_mask(which), NT)

            def load(index):
                block = bias_rows(bias, head, tiles, tile, index // 2)
                at = (index % 2) * CHUNK
                return scores[which, pl.ds(index * CHUNK, CHUNK), :] + block[at : at + CHUNK]

            def low_out(index, value):
                low_probs[which, pl.ds(index * CHUNK, CHUNK), :] = value

            total, log_total = softmax_chunks(load, seen // CHUNK, low_out)
            lse[pl.ds(head, 1), rows] = log_total
            value = values_turned[which * DH : (which + 1) * DH, :seen]
            made.append(dot(value, low_probs[which, pl.ds(0, seen), :]) * (1.0 / total))
        made = jnp.concatenate(made, axis=0)
        o1_turned[lanes_at(0, pair), rows] = made
        o1[rows, lanes_at(0, pair)] = turn(made.astype(BF), eye)
        between()


def inner_rows(pair, which, o_turned, do_turned):
    here = pl.ds(pair * 128 + which * DH, DH)
    upstream = do_turned[which * DH : (which + 1) * DH, :].astype(F32)
    return eight_rows(jnp.sum(o_turned[here, :] * upstream, axis=0, keepdims=True))


def self_backward(
    pair, qkv, bias, lse, o1_turned, do1, dqkv, buckets, bias_total, eye,
    scores, dprobs, low_probs, low_dscores, between,
):
    width = do1.shape[1]
    length = qkv.shape[0]
    tiles = length // 128
    keys_turned = turn(qkv[:, lanes_at(width, pair)], eye)
    do_turned = turn(do1[:, lanes_at(0, pair)], eye)
    queries, upstreams = [], []
    for tile in range(tiles // 2):
        rows, seen = pl.ds(tile * 256, 256), (tile + 1) * 256
        query = qkv[rows, lanes_at(0, pair)]
        key = qkv[pl.ds(0, seen), lanes_at(width, pair)]
        value = qkv[pl.ds(0, seen), lanes_at(2 * width, pair)]
        upstream = do1[rows, lanes_at(0, pair)]
        made = []
        for which in range(2):
            head = 2 * pair + which
            at = pl.ds((2 * tile + which) * 256, 256)
            queries.append(query * head_mask(which))
            upstreams.append(upstream * head_mask(which))
            inner = inner_rows(pair, which, o1_turned.at[:, rows], do_turned[:, tile * 256 : seen])
            scores[which, pl.ds(0, seen), :] = dot(key, queries[-1], NT)
            dprobs[which, pl.ds(0, seen), :] = dot(value, upstreams[-1], NT)
            log_total = eight_rows(lse[pl.ds(head, 1), rows])
            for index in range(seen // CHUNK):
                here = pl.ds(index * CHUNK, CHUNK)
                block = bias_rows(bias, head, tiles, tile, index // 2)
                start = (index % 2) * CHUNK
                value_here = scores[which, here, :] + block[start : start + CHUNK]
                low_probs[here, at], low_dscores[here, at] = back_chunk(
                    value_here, dprobs[which, here, :], log_total, inner
                )
            made.append(
                dot(keys_turned[which * DH : (which + 1) * DH, :seen], low_dscores[pl.ds(0, seen), at])
            )
        dqkv[rows, lanes_at(0, pair)] = turn(jnp.concatenate(made, axis=0).astype(BF), eye)
        between()
    queries = jnp.concatenate(queries, axis=0)
    upstreams = jnp.concatenate(upstreams, axis=0)
    for tile in range(tiles // 2):
        rows, later = pl.ds(tile * 256, 256), pl.ds(tile * 512, 2 * length - tile * 512)
        dkey = dot(low_dscores[rows, later], queries[tile * 512 :])
        dqkv[rows, lanes_at(width, pair)] = dkey.astype(BF)
        dvalue = dot(low_probs[rows, later], upstreams[tile * 512 :])
        dqkv[rows, lanes_at(2 * width, pair)] = dvalue.astype(BF)
    for which in range(2):
        total = jnp.zeros((8, 128), F32)
        for away in range(tiles):
            summed = None
            for key in range(tiles - away):
                query = key + away
                start = (2 * (query // 2) + which) * 256 + (query % 2) * 128
                block = low_dscores[pl.ds(key * 128, 128), pl.ds(start, 128)].astype(F32)
                summed = block if summed is None else summed + block
            total = total + lax.dot_general(
                diagonal_sums(summed), buckets[away].astype(F32), (NN, ((), ())), precision=HIGHEST,
                preferred_element_type=F32,
            )
        row = lax.broadcasted_iota(jnp.int32, (8, 128), 0)
        bias_total[...] += jnp.where(row == 2 * pair + which, total, 0.0)


def diagonal_sums(tile):
    wide = jnp.concatenate([tile, jnp.zeros_like(tile)], axis=1)
    turned = wide[0:8]
    for group in range(1, 16):
        turned = turned + pltpu.roll(wide[8 * group : 8 * group + 8], 256 - 8 * group, 1)
    place_in = lax.broadcasted_iota(jnp.int32, (8, 256), 0)
    for bit in (1, 2, 4):
        moved = pltpu.roll(turned, 256 - bit, 1)
        turned = jnp.where(lax.rem(place_in // bit, 2) == 1, moved, turned)
    return jnp.broadcast_to(jnp.sum(turned, axis=0, keepdims=True), (8, 256))


def lane_row(index):
    lane = lax.broadcasted_iota(jnp.int32, (1, 128), 1)
    return jnp.where(lane == index, 1.0, 0.0).astype(BF)


def with_mask(key, mask, which):
    spot = lane_row((1 - which) * DH)
    return key * (1 - spot) + mask * spot


def with_one(query, which):
    return query * head_mask(which) + lane_row((1 - which) * DH)


def cross_forward(pair, q2, kc, vc, mask, o2, o2_turned, lse, eye, scores, low_probs, between):
    values_turned = turn(vc[:, lanes_at(0, pair)], eye)
    key = kc[:, lanes_at(0, pair)]
    keys = [with_mask(key, mask[...], which) for which in range(2)]
    for tile in range(q2.shape[0] // 256):
        rows = pl.ds(tile * 256, 256)
        query = q2[rows, lanes_at(0, pair)]
        made = []
        for which in range(2):
            scores[which] = dot(keys[which], with_one(query, which), NT)

            def load(index):
                return scores[which, pl.ds(index * CHUNK, CHUNK), :]

            def low_out(index, value):
                low_probs[which, pl.ds(index * CHUNK, CHUNK), :] = value

            total, log_total = softmax_chunks(load, key.shape[0] // CHUNK, low_out)
            lse[pl.ds(2 * pair + which, 1), rows] = log_total
            value = values_turned[which * DH : (which + 1) * DH, :]
            made.append(dot(value, low_probs[which]) * (1.0 / total))
        made = jnp.concatenate(made, axis=0)
        o2_turned[lanes_at(0, pair), rows] = made
        o2[rows, lanes_at(0, pair)] = turn(made.astype(BF), eye)
        between()


def cross_backward(
    pair, q2, kc, vc, mask, lse, o2_turned, do2, dq2, dkc, dvc, eye,
    scores, dprobs, low_probs, low_dscores, between,
):
    key, value = kc[:, lanes_at(0, pair)], vc[:, lanes_at(0, pair)]
    keys = [with_mask(key, mask[...], which) for which in range(2)]
    keys_turned = turn(key, eye)
    do_turned = turn(do2[:, lanes_at(0, pair)], eye)
    queries, upstreams = [], []
    for tile in range(q2.shape[0] // 256):
        rows = pl.ds(tile * 256, 256)
        query, upstream = q2[rows, lanes_at(0, pair)], do2[rows, lanes_at(0, pair)]
        made = []
        for which in range(2):
            at = pl.ds((2 * tile + which) * 256, 256)
            queries.append(query * head_mask(which))
            upstreams.append(upstream * head_mask(which))
            inner = inner_rows(
                pair, which, o2_turned.at[:, rows], do_turned[:, tile * 256 : (tile + 1) * 256]
            )
            scores[which] = dot(keys[which], with_one(query, which), NT)
            dprobs[which] = dot(value, upstreams[-1], NT)
            log_total = eight_rows(lse[pl.ds(2 * pair + which, 1), rows])
            for index in range(key.shape[0] // CHUNK):
                here = pl.ds(index * CHUNK, CHUNK)
                low_probs[here, at], low_dscores[here, at] = back_chunk(
                    scores[which, here, :], dprobs[which, here, :], log_total, inner
                )
            made.append(dot(keys_turned[which * DH : (which + 1) * DH, :], low_dscores[:, at]))
        dq2[rows, lanes_at(0, pair)] = turn(jnp.concatenate(made, axis=0).astype(BF), eye)
        between()
    dkc[:, lanes_at(0, pair)] = dot(low_dscores[...], jnp.concatenate(queries, axis=0)).astype(BF)
    dvc[:, lanes_at(0, pair)] = dot(low_probs[...], jnp.concatenate(upstreams, axis=0)).astype(BF)


def row_tiles(length):
    def run(step):
        for tile in range(length // 64):
            step(tile)

    return run


def rows_of(tile):
    return pl.ds(tile * 64, 64)


def back_through_norm(values, gain, upstream):
    scale = lax.rsqrt(jnp.mean(values * values, axis=-1, keepdims=True) + norm_eps)
    weighted = upstream * gain
    inner = jnp.mean(weighted * values, axis=-1, keepdims=True)
    return (
        scale * weighted - values * (scale * scale * scale * inner),
        jnp.sum(upstream * values * scale, axis=0, keepdims=True),
    )


def feed_tile(
    tile, h3, df, h3_turned, df_turned, feed, y_part, dn_part, g_feed, width,
    gate_up, dhidden, hidden, dpair,
):
    up_down = columns_of(feed, tile, 0, 2 * width)
    down = columns_of(feed, tile, 2 * width, width)
    gate_up[...] = dot(h3[...], up_down)
    dhidden[...] = dot(df[...], down)
    root = math.sqrt(2.0 / math.pi)

    @row_tiles(h3.shape[0])
    def _(index):
        rows = rows_of(index)
        gate, upper = gate_up[rows, pl.ds(0, width)], gate_up[rows, pl.ds(width, width)]
        upstream = dhidden[rows, :]
        square = gate * gate
        curve = jnp.tanh(gate * (root + root * 0.044715 * square))
        half = 0.5 + 0.5 * curve
        active = gate * half
        slope = half + 0.5 * gate * (1.0 - curve * curve) * (root + root * 3 * 0.044715 * square)
        hidden[rows, :] = (active * upper).astype(BF)
        dpair[rows, pl.ds(0, width)] = (upstream * upper * slope).astype(BF)
        dpair[rows, pl.ds(width, width)] = (upstream * active).astype(BF)

    y_now = dot(hidden[...], down, NT)
    dn_now = dot(dpair[...], up_down, NT)
    if tile == 0:
        y_part[...] = y_now
        dn_part[...] = dn_now
    else:
        y_part[...] += y_now
        dn_part[...] += dn_now
    put_columns(g_feed, tile, 0, dot(h3_turned[...], dpair[...]))
    put_columns(g_feed, tile, 2 * width, dot(df_turned[...], hidden[...]))


FEED_TILE = 256
PIECE = 768


def columns_of(ref, piece, start, count):
    value = ref[piece, :, :, :, pl.ds(start, count)]
    return value.reshape(value.shape[0] * value.shape[1] * value.shape[2], count)


def put_columns(ref, piece, start, value):
    ref[piece, :, :, :, pl.ds(start, value.shape[1])] = value.astype(ref.dtype).reshape(
        ref.shape[1:4] + (value.shape[1],)
    )


FRONT_OUT = (
    "near", "bias", "h1", "qkv", "lse1", "o1", "o1_turned", "x1", "h2", "q2", "enc_mine", "kc", "vc",
    "mask", "lse2", "o2", "o2_turned", "dx2", "g_feed", "layer_out", "stats",
)


def front_kernel(
    levels, slots,
    self_proj, self_out, cross_proj, cross_out, feed_in, feed_out, encoder, tok_own, grad_own,
    gains, bias_table, one_hot, blank, items, lengths, limit, *refs,
):
    outs = dict(zip(FRONT_OUT, refs))
    slot_of = refs[len(FRONT_OUT)]
    refs = refs[len(FRONT_OUT) + 1 :]
    kept = dict(zip(FRONT_OUT, refs))
    (
        near, bias, h1, qkv, lse1, o1, o1_turned, x1, h2, q2, enc_mine, kc, vc, mask, lse2, o2,
        o2_turned, dx2, g_feed, layer_out, stats,
    ) = refs[: len(FRONT_OUT)]
    (
        scores, low_probs, gate_up, dhidden, hidden, dpair, feed, enc, info, scalars, tok, grad,
        part_one, part_two, y_part, dn_part, got_one, got_two, got_y, got_dn, x2, h3, df, h3_turned,
        df_turned, eye, strips, send, recv, local,
    ) = refs[len(FRONT_OUT) :]
    place = Place(levels)
    enter(place.partners())
    copies, moves = Copies(send, recv), Moves(local)
    length, width = o1.shape
    half_rows = length // 2
    keep = lambda *names: [moves.start(name, kept[name], outs[name]) for name in names]
    tok_sent = copies.remote(tok_own, tok.at[place.core], place.sibling)

    def pack(piece, start, value):
        target = near if piece < near.shape[0] else feed
        at = pl.ds(start, value.shape[1])
        target[piece % near.shape[0], place.a, place.p, :, at] = value.astype(BF)

    for base, proj, out in ((0, self_proj, self_out), (2, cross_proj, cross_out)):
        pack(base, 0, proj[0])
        pack(base, width, proj[1])
        pack(base + 1, 0, proj[2])
        pack(base + 1, width, out[...])
    row = lax.broadcasted_iota(jnp.int32, (8, 128), 0)
    lane = lax.broadcasted_iota(jnp.int32, (8, 128), 1)
    known = jnp.zeros((8, 128), jnp.int32)
    per_chip = enc.shape[3]
    for index in range(per_chip):
        pair = jnp.where(lane == 0, items[index], jnp.where(lane == 1, lengths[index], 0))
        known = jnp.where(row == index, pair, known)
    info[place.a, place.p] = known
    half_cols = enc.shape[5]
    own_cols = pl.ds(pl.multiple_of(place.core * half_cols, half_cols), half_cols)
    enc[place.core, place.a, place.p] = encoder[:, own_cols].reshape(per_chip, KB, half_cols)
    for tile in range(feed.shape[0]):
        at = pl.ds(tile * FEED_TILE, FEED_TILE)
        pack(4 + tile, 0, feed_in[0, :, at])
        pack(4 + tile, FEED_TILE, feed_in[1, :, at])
        pack(4 + tile, 2 * FEED_TILE, feed_out[:, at])

    pump = Pump("ends", 1.5)

    def piece(index):
        target = near if index < near.shape[0] else feed
        return gather_chain(
            place, copies, lambda a, p: target.at[index % near.shape[0], a, p],
            plane_first=index == 3,
        )

    pieces = [piece(index) for index in range(near.shape[0] + feed.shape[0])]
    info_chain = gather_chain(place, copies, lambda a, p: info.at[a, p])
    enc_chain = gather_chain(place, copies, lambda a, p: enc.at[place.core, a, p])
    pump.add(info_chain, pieces[0], pieces[1], enc_chain, pieces[3], pieces[2], *pieces[4:])
    grad_sent = copies.remote(grad_own, grad.at[place.core], place.sibling)
    tok[place.core] = tok_own[...]
    grad[place.core] = grad_own[...]
    lse1[...] = jnp.zeros_like(lse1)
    lse2[...] = jnp.zeros_like(lse2)
    make_eye(eye)
    heads = width // DH
    strips[pl.ds(0, bias_table.shape[0]), :] = blank[...] + lax.dot_general(
        bias_table[...], one_hot[...], (NN, ((), ())), precision=HIGHEST, preferred_element_type=F32
    )
    tiles = length // 128
    for head in range(heads):
        for tile in range(tiles):
            strip = strips[pl.ds(place.core * heads + head, 1), pl.ds(tile * 256, 256)]
            rows = jnp.broadcast_to(strip, (128, 256))
            bias[head * tiles + tile] = pltpu.roll(rows, 0, 1, stride=1, stride_axis=0)[:, :128]
    keep("bias")
    pump.work(3.0)
    tok_sent.wait_recv()

    @row_tiles(length)
    def _(tile):
        part = tile // (half_rows // 64)
        values = tok[part, rows_of(tile - part * (half_rows // 64)), :].astype(F32)
        h1[rows_of(tile), :] = norm_rows(values, gains[0:1, :]).astype(BF)

    keep("h1")
    pump.work(2.0)
    pump.until(pieces[0])
    qkv[:, pl.ds(0, 2 * width)] = dot(h1[...], columns_of(near, 0, 0, 2 * width)).astype(BF)
    pump.work(2.0)
    pump.until(pieces[1])
    qkv[:, pl.ds(2 * width, width)] = dot(h1[...], columns_of(near, 1, 0, width)).astype(BF)
    keep("qkv")
    pump.work(1.0)
    for pair in range(width // 128):
        self_forward(
            pair, qkv, bias, o1, o1_turned, lse1, eye, scores, low_probs, lambda: pump.work(1.5)
        )
    keep("lse1", "o1", "o1_turned")
    part_one[...] = dot(o1[...], columns_of(near, 1, width, width), NT)
    one_sent = copies.remote(part_one, got_one, place.sibling)
    pump.work(1.0)
    pump.until(enc_chain)
    enc_sent = copies.remote(enc.at[place.core], enc.at[place.core], place.sibling)
    pump.until(info_chain)
    moves.start("info", info, scalars)
    pump.work(2.0)
    one_sent.wait_recv()

    @row_tiles(length)
    def _(tile):
        rows = rows_of(tile)
        part = tile // (half_rows // 64)
        values = tok[part, rows_of(tile - part * (half_rows // 64)), :].astype(F32)
        values = values + (part_one[rows, :] + got_one[rows, :])
        x1[rows, :] = values
        h2[rows, :] = norm_rows(values, gains[1:2, :]).astype(BF)

    keep("x1", "h2")
    moves.need("info")
    total_blocks = enc.shape[1] * 4 * per_chip

    def block_at(block):
        chip = block // per_chip
        return (chip // 4, lax.rem(chip, 4), lax.rem(block, per_chip))

    def look(block, carried):
        count, found, sizes = carried
        z, p, at = block_at(block)
        own = (scalars[z, p, at, 0] == place.me).astype(jnp.int32)
        slot_of[block] = own * count + (1 - own) * slots
        here = [own * (count == index).astype(jnp.int32) for index in range(slots)]
        found = tuple(known + each * block for known, each in zip(found, here))
        sizes = tuple(known + each * scalars[z, p, at, 1] for known, each in zip(sizes, here))
        return (count + own, found, sizes)

    nothing = (jnp.int32(0),) * slots
    _, found, sizes = lax.fori_loop(0, total_blocks, look, (jnp.int32(0), nothing, nothing))
    pump.work(3.0)
    pump.until(pieces[2])
    pump.until(pieces[3])
    keep("near")
    enc_sent.wait_recv()
    place_in = lax.broadcasted_iota(jnp.int32, (KB, 128), 0)
    for index in range(slots):
        here = pl.ds(index * KB, KB)
        z, p, at = block_at(found[index])
        for half in range(2):
            enc_mine[here, pl.ds(half * half_cols, half_cols)] = enc[half, z, p, at]
        mask[here, :] = jnp.where(place_in < sizes[index], 0.0, masked_score).astype(BF)
    keep("enc_mine", "mask")
    pump.work(1.0)
    q2[...] = dot(h2[...], columns_of(near, 2, 0, width)).astype(BF)
    kc[...] = dot(enc_mine[...], columns_of(near, 2, width, width)).astype(BF)
    vc[...] = dot(enc_mine[...], columns_of(near, 3, 0, width)).astype(BF)
    keep("q2", "kc", "vc")
    pump.work(4.0)
    for pair in range(width // 128):
        cross_forward(
            pair, q2, kc, vc, mask, o2, o2_turned, lse2, eye, scores, low_probs,
            lambda: pump.work(2.5),
        )
    keep("lse2", "o2", "o2_turned")
    part_two[...] = dot(o2[...], columns_of(near, 3, width, width), NT)
    two_sent = copies.remote(part_two, got_two, place.sibling)
    pump.work(1.0)
    grad_sent.wait_recv()
    top = limit[0]

    @row_tiles(length)
    def _(tile):
        part = tile // (half_rows // 64)
        rows = rows_of(tile)
        row = lax.broadcasted_iota(jnp.int32, (64, 1), 0) + tile * 64
        values = grad[part, rows_of(tile - part * (half_rows // 64)), :].astype(F32)
        df[rows, :] = jnp.where(row < top, values, 0.0).astype(BF)

    two_sent.wait_recv()

    @row_tiles(length)
    def _(tile):
        rows = rows_of(tile)
        values = x1[rows, :] + (part_two[rows, :] + got_two[rows, :])
        x2[rows, :] = values
        h3[rows, :] = norm_rows(values, gains[2:3, :]).astype(BF)

    h3_turned[...] = turn(h3[...], eye)
    df_turned[...] = turn(df[...], eye)
    pump.work(4.0)
    for tile in range(feed.shape[0]):
        pump.until(pieces[4 + tile])
        feed_tile(
            tile, h3, df, h3_turned, df_turned, feed, y_part, dn_part, g_feed,
            FEED_TILE, gate_up, dhidden, hidden, dpair,
        )
        moves.start(("g_feed", tile), g_feed.at[tile], outs["g_feed"].at[tile])
        pump.work(5.0)
    pump.drain()
    dn_sent = copies.remote(dn_part, got_dn, place.sibling)
    other_rows = pl.ds(pl.multiple_of((1 - place.core) * half_rows, half_rows), half_rows)
    y_sent = copies.remote(y_part.at[other_rows, :], got_y, place.sibling)
    dn_sent.wait_recv()
    stats[...] = jnp.zeros_like(stats)

    @row_tiles(length)
    def _(tile):
        rows = rows_of(tile)
        delta, gain = back_through_norm(
            x2[rows, :], gains[2:3, :], dn_part[rows, :] + got_dn[rows, :]
        )
        dx2[rows, :] = df[rows, :].astype(F32) + delta
        stats[0:1, :] += gain

    keep("dx2")
    y_sent.wait_recv()

    @row_tiles(half_rows)
    def _(tile):
        rows = rows_of(tile)
        start = pl.multiple_of(place.core * half_rows + tile * 64, 64)
        here = pl.ds(start, 64)
        values = x2[here, :] + (y_part[here, :] + got_y[rows, :])
        layer_out[rows, :] = values.astype(BF)
        row = lax.broadcasted_iota(jnp.int32, (64, 1), 0) + start
        stats[1:2, :] += jnp.sum(jnp.where(row < top, values * values, 0.0), axis=0, keepdims=True)

    keep("layer_out", "stats")
    moves.finish()
    copies.finish()


def front_shapes(blocks, slots, length, width, rows, pieces):
    long = blocks // 4
    heads = width // DH
    tiles = length // 128
    keys = slots * KB
    return {
        "near": ((pieces, long, 4, rows, PIECE), BF),
        "bias": ((heads * tiles, 128, 128), F32),
        "h1": ((length, D), BF),
        "qkv": ((length, 3 * width), BF),
        "lse1": ((8, length), F32),
        "o1": ((length, width), BF),
        "o1_turned": ((width, length), F32),
        "x1": ((length, D), F32),
        "h2": ((length, D), BF),
        "q2": ((length, width), BF),
        "enc_mine": ((keys, D), BF),
        "kc": ((keys, width), BF),
        "vc": ((keys, width), BF),
        "mask": ((keys, 128), BF),
        "lse2": ((8, length), F32),
        "o2": ((length, width), BF),
        "o2_turned": ((width, length), F32),
        "dx2": ((length, D), F32),
        "g_feed": ((pieces, long, 4, rows, PIECE), BF),
        "layer_out": ((length // 2, D), BF),
        "stats": ((8, D), F32),
    }


SMEM = pl.BlockSpec(memory_space=pltpu.SMEM)


def front(blocks, slots, shapes, operands, scalars, per_chip):
    levels = int(math.log2(blocks)) - 2
    long = blocks // 4
    length = shapes["h1"][0][0]
    pieces, rows = shapes["near"][0][0], shapes["near"][0][3]
    keys = slots * KB
    count = (2 * pieces + 2) * (levels + 3) + 8
    outs = tuple(jax.ShapeDtypeStruct(*shapes[name]) for name in FRONT_OUT)
    wide = pltpu.VMEM((length, D), F32)
    low = pltpu.VMEM((length, D), BF)
    return pl.pallas_call(
        functools.partial(front_kernel, levels, slots),
        out_shape=outs + (jax.ShapeDtypeStruct((blocks * per_chip,), jnp.int32),),
        in_specs=[VMEM] * len(operands) + [SMEM] * len(scalars),
        out_specs=(ANY,) * len(outs) + (SMEM,),
        scratch_shapes=[pltpu.VMEM(*shapes[name]) for name in FRONT_OUT]
        + [
            pltpu.VMEM((2, keys, 256), F32),
            pltpu.VMEM((2, keys, 256), BF),
            pltpu.VMEM((length, 2 * FEED_TILE), F32),
            pltpu.VMEM((length, FEED_TILE), F32),
            pltpu.VMEM((length, FEED_TILE), BF),
            pltpu.VMEM((length, 2 * FEED_TILE), BF),
            pltpu.VMEM(*shapes["near"]),
            pltpu.VMEM((2, long, 4, per_chip, KB, D // 2), BF),
            pltpu.VMEM((long, 4, 8, 128), jnp.int32),
            pltpu.SMEM((long, 4, 8, 128), jnp.int32),
            pltpu.VMEM((2, length // 2, D), BF),
            pltpu.VMEM((2, length // 2, D), BF),
            wide, wide, wide, wide, wide, wide,
            pltpu.VMEM((length // 2, D), F32),
            wide, wide, low, low,
            pltpu.VMEM((D, length), BF),
            pltpu.VMEM((D, length), BF),
            pltpu.VMEM((256, 256), BF),
            pltpu.VMEM((16, 256 * (length // 128)), F32),
            pltpu.SemaphoreType.DMA((count,)),
            pltpu.SemaphoreType.DMA((count,)),
            pltpu.SemaphoreType.DMA((len(FRONT_OUT) + pieces + 1,)),
        ],
        compiler_params=pltpu.CompilerParams(
            collective_id=0, has_side_effects=True, vmem_limit_bytes=int(63.4 * 2**20)
        ),
    )(*operands, *scalars)


BACK_IN = (
    "g_feed", "near", "dx2", "o2", "q2", "kc", "vc", "mask", "lse2", "o2_turned", "h2", "x1",
    "o1", "qkv", "bias", "lse1", "o1_turned", "h1", "stats",
)


def put_outer(ref, piece, start, left, right, eye):
    long, half = ref.shape[1] // 2, D // 2
    for index in range(2):
        turned = turn(left[:, pl.ds(index * half, half)].astype(BF), eye)
        value = dot(turned, right).astype(BF)
        value = value.reshape((long,) + ref.shape[2:4] + (value.shape[1],))
        ref[piece, pl.ds(long * index, long), :, :, pl.ds(start, value.shape[3])] = value


def put_rows(ref, left, right, dims, add=False):
    for start in range(0, ref.shape[0], 256):
        rows = pl.ds(start, 256)
        value = dot(left[rows, :].astype(BF), right, dims)
        ref[rows, :] = (ref[rows, :] + value if add else value).astype(ref.dtype)


def back_kernel(
    levels, slots,
    gains, tok_own, buckets, slot_of, limit, enc_kept, *refs,
):
    sources = dict(zip(BACK_IN, refs))
    grad_out, decoder_grad, encoder_grad, sums, squares = refs[len(BACK_IN) : len(BACK_IN) + 5]
    refs = refs[len(BACK_IN) + 5 :]
    landed = dict(zip(BACK_IN, refs))
    (
        g_feed, near, dx2, o2, q2, kc, vc, mask, lse2, o2_turned, h2, x1, o1, qkv, bias, lse1,
        o1_turned, h1, stats,
    ) = refs[: len(BACK_IN)]
    (
        g_near, two, one, total, zs, line_two, line_one, line_total, line_zs, spread, e_two, e_one,
        e_total, e_zs, do, dq, dkc, dvc, dqkv, e_all, e_got, part, got_dn, got_half,
        bias_total, small, small_plane, small_middle, small_line, last, last_plane, last_middle,
        last_line, eye, scores, dprobs, low_probs, low_dscores, free, send, recv, local,
    ) = refs[len(BACK_IN) :]
    place = Place(levels)
    copies, moves = Copies(send, recv), Moves(local)
    near_pieces = near.shape[0]
    for name in BACK_IN:
        moves.start(name, sources[name], landed[name])
    enter(place.mates())
    pump = Pump("xy", 4.0)
    length, width = o1.shape
    half_rows = length // 2
    top = limit[0]
    half_cols = e_all.shape[3]

    def piece(index):
        source = View(g_near if index < near_pieces else g_feed, index % near_pieces)
        out = View(grad_out, index)
        if index == near_pieces:
            scratch = [View(ref) for ref in (line_two, line_one, line_total, line_zs)]
            return scatter_line_first(place, copies, source, *scratch, out)
        at = spot[index]
        scratch = [View(ref, at) for ref in (two, one, total, zs)]
        return scatter_chain(place, copies, source, *scratch, out)

    def half_piece(index, start):
        columns = pl.ds(start, width)
        scratch = [View(ref, spot[index], columns=columns) for ref in (two, one, total, zs)]
        return scatter_chain(
            place, copies, View(g_near, index, columns=columns), *scratch,
            View(grad_out, index, columns=columns),
        )

    spot = {5: 0, 6: 1, 7: 2, 2: 3, 3: 4, 0: 0, 1: 1}

    moves.need("g_feed")
    feed_chains = [piece(index) for index in range(near_pieces, near_pieces + g_feed.shape[0])]
    pump.add(*feed_chains)
    make_eye(eye)
    moves.need("near", "dx2", "o2")
    put_rows(do, dx2, columns_of(near, 3, width, width), NN)
    put_outer(g_near, 3, width, dx2, o2[...], eye)
    pump.work(2.5)
    moves.need("q2", "kc", "vc", "mask", "lse2", "o2_turned")
    for pair in range(width // 128):
        cross_backward(
            pair, q2, kc, vc, mask, lse2, o2_turned, do, dq, dkc, dvc, eye,
            scores, dprobs, low_probs, low_dscores, lambda: pump.work(4.0),
        )
    enc_mine = low_probs.at[:, pl.ds(0, D)]
    moves.start("enc_mine", enc_kept, enc_mine)
    pump.work(2.0)
    put_rows(part, dq, columns_of(near, 2, 0, width), NT)
    dn_sent = copies.remote(part, got_dn, place.sibling)
    half_long = near.shape[1] // 2
    for index in range(2):
        weights = [
            near[piece, half_long * index : half_long * (index + 1), :, :, pl.ds(start, width)]
            .reshape(half_cols, width)
            for piece, start in ((2, width), (3, 0))
        ]
        for first in range(0, slots, 6):
            keys = pl.ds(first * KB, 6 * KB)
            term = dot(dkc[keys, :], weights[0], NT) + dot(dvc[keys, :], weights[1], NT)
            e_all[index, pl.ds(first, 6)] = term.astype(BF).reshape(6, KB, half_cols)

    e_sent = copies.remote(
        e_all.at[1 - place.core, pl.ds(0, slots)], e_got, place.sibling
    )
    pump.work(2.0)
    moves.need("h2")
    put_outer(g_near, 2, 0, h2, dq[...], eye)
    moves.need("enc_mine")
    put_outer(g_near, 2, width, low_probs, dkc[...], eye)
    pump.work(1.5)
    put_outer(g_near, 3, 0, low_probs, dvc[...], eye)
    pump.work(1.5)
    pump.add(piece(2), piece(3))
    e_sent.wait_recv()

    for index in range(slots):
        own = e_all[place.core, index].astype(F32)
        e_all[place.core, index] = (own + e_got[index].astype(F32)).astype(BF)

    e_all[place.core, slots] = jnp.zeros((KB, half_cols), BF)
    per_chip = spread.shape[2] // KB
    for block in range(spread.shape[0] * 4 * per_chip):
        chip, at = block // per_chip, block % per_chip
        spread[chip // 4, chip % 4, pl.ds(at * KB, KB), :] = e_all[place.core, slot_of[block]]
    scratch = [View(ref) for ref in (spread, e_two, e_one, e_total, e_zs, encoder_grad)]
    pump.add(scatter_chain(place, copies, *scratch))
    moves.need("x1")
    dn_sent.wait_recv()
    sums[...] = jnp.zeros_like(sums)
    bias_total[...] = jnp.zeros_like(bias_total)

    @row_tiles(length)
    def _(tile):
        rows = rows_of(tile)
        delta, gain = back_through_norm(x1[rows, :], gains[1:2, :], part[rows, :] + got_dn[rows, :])
        dx2[rows, :] = dx2[rows, :] + delta
        sums[1:2, :] += 0.5 * gain

    pump.work(4.0)
    moves.need(*BACK_IN)
    put_rows(do, dx2, columns_of(near, 1, width, width), NN)
    put_outer(g_near, 1, width, dx2, o1[...], eye)
    pump.work(2.5)
    pump.until(feed_chains[1])
    pump.until(feed_chains[2])
    writers = [place.first, place.second] + [place.partner(level) for level in range(levels)]
    for device in writers:
        pl.semaphore_signal(free, inc=1, device_id=device, device_id_type=MESH)
    pl.semaphore_wait(free, len(writers))
    pump.add(half_piece(1, width))
    for pair in range(width // 128):
        self_backward(
            pair, qkv, bias, lse1, o1_turned, do, dqkv, buckets, bias_total, eye,
            scores, dprobs, low_probs, low_dscores, lambda: pump.work(2.5),
        )
    pump.work(1.0)
    put_outer(g_near, 0, 0, h1, dqkv[:, pl.ds(0, 2 * width)], eye)
    pump.add(half_piece(0, 0), half_piece(0, width))
    pump.work(1.0)
    put_outer(g_near, 1, 0, h1, dqkv[:, pl.ds(2 * width, width)], eye)
    pump.add(half_piece(1, 0))
    copies.left(dn_sent)
    wide = pl.ds(0, 2 * width), pl.ds(2 * width, width)
    for index, columns in enumerate(wide):
        weights = columns_of(near, index, 0, columns.size)
        put_rows(part, dqkv.at[:, columns], weights, NT, add=index > 0)
    own_rows = pl.multiple_of(place.core * half_rows, half_rows)
    other_rows = pl.ds(pl.multiple_of((1 - place.core) * half_rows, half_rows), half_rows)
    half_sent = copies.remote(part.at[other_rows, :], got_half, place.sibling)
    pump.work(3.0)
    half_sent.wait_recv()
    sums[2:3, :] = 0.5 * stats[0:1, :]
    sums[3:4, :] = stats[1:2, :]

    @row_tiles(half_rows)
    def _(tile):
        rows = rows_of(tile)
        start = pl.multiple_of(own_rows + tile * 64, 64)
        here = pl.ds(start, 64)
        values = tok_own[rows, :].astype(F32)
        delta, gain = back_through_norm(values, gains[0:1, :], part[here, :] + got_half[rows, :])
        result = dx2[here, :] + delta
        decoder_grad[rows, :] = result
        row = lax.broadcasted_iota(jnp.int32, (64, 1), 0) + start
        sums[0:1, :] += gain
        sums[4:5, :] += jnp.sum(jnp.where(row < top, result * result, 0.0), axis=0, keepdims=True)
        sums[5:6, :] += jnp.sum(jnp.where(row < top, 1.0, 0.0), axis=0, keepdims=True) * jnp.ones((1, D), F32)

    rows_bias = bias_total[...]
    for index in range(2):
        keep = jnp.where(place.core == index, 1.0, 0.0)
        sums[pl.ds(8 + 8 * index, 8), pl.ds(0, 128)] = rows_bias * keep
    small[...] = sums[...]
    pump.add(sum_chain(place, copies, small, small_plane, small_middle, small_line, sums))
    pump.drain()
    square = jnp.zeros((8, 128), F32)
    for index in range(grad_out.shape[0]):
        for start in range(0, PIECE, 128):
            tile = grad_out[index, :, pl.ds(start, 128)]
            tile = tile * tile
            for row in range(0, tile.shape[0], 8):
                square = square + tile[row : row + 8]
    last[...] = square
    pump.add(sum_chain(place, copies, last, last_plane, last_middle, last_line, squares))
    pump.drain()
    copies.finish()


def back(blocks, slots, shapes, made, tok_own, gains, limit, buckets, key_rows):
    levels = int(math.log2(blocks)) - 2
    long = blocks // 4
    pieces, rows = shapes["near"][0][0], shapes["near"][0][3]
    length, width = shapes["o1"][0]
    keys = slots * KB
    half = D // 2
    by_name = dict(zip(FRONT_OUT, made))
    count = (2 * pieces + 3) * (levels + 3) + 3 + 2 * (7 + long - 1)
    shape = lambda *dims: jax.ShapeDtypeStruct(dims, F32)
    outs = (
        shape(2 * pieces, rows, PIECE),
        shape(length // 2, D),
        shape(key_rows, half),
        shape(24, D),
        shape(8, 128),
    )
    steps = 2**levels - 1
    usual = 5
    block = (rows, PIECE)
    enc_block = (key_rows, half)
    sizes = [shapes["near"]]
    sizes += [((usual,) + lead + block, BF) for lead in ((2, long), (long,), (long,), (steps,))]
    sizes += [(lead + block, BF) for lead in ((2,), (), (long // 2, 4), (steps, 4))]
    sizes += [
        (lead + enc_block, BF) for lead in ((long, 4), (2, long), (long,), (long,), (steps,))
    ]
    sizes += [
        ((length, width), BF), ((length, width), BF), ((keys, width), BF), ((keys, width), BF),
        ((length, 3 * width), BF), ((2, slots + 1, KB, half), BF),
        ((slots, KB, half), BF), ((length, D), F32), ((length, D), F32), ((length // 2, D), F32),
        ((8, 128), F32),
    ]
    for member in ((24, D), (8, 128)):
        sizes += [(lead + member, F32) for lead in ((), (8,), (), (long,))]
    sizes += [
        ((256, 256), BF), ((2, keys, 256), F32), ((2, keys, 256), F32), ((keys, 2 * length), BF),
        ((keys, 2 * length), BF),
    ]
    return pl.pallas_call(
        functools.partial(back_kernel, levels, slots),
        out_shape=outs,
        in_specs=[VMEM, VMEM, VMEM, SMEM, SMEM] + [ANY] * (len(BACK_IN) + 1),
        out_specs=(VMEM,) * 5,
        scratch_shapes=[pltpu.VMEM(*shapes[name]) for name in BACK_IN]
        + [pltpu.VMEM(*size) for size in sizes]
        + [
            pltpu.SemaphoreType.REGULAR,
            pltpu.SemaphoreType.DMA((count,)),
            pltpu.SemaphoreType.DMA((count,)),
            pltpu.SemaphoreType.DMA((len(BACK_IN) + 1,)),
        ],
        compiler_params=pltpu.CompilerParams(
            collective_id=1, has_side_effects=True, vmem_limit_bytes=int(63.4 * 2**20)
        ),
    )(
        gains, tok_own, buckets, made[-1], limit, by_name["enc_mine"],
        *(by_name[name] for name in BACK_IN),
    )


def adam_kernel(grads, sums, squares, *refs):
    params, firsts, seconds, passed = refs[:8], refs[8:16], refs[16:24], refs[24:27]
    news, new_firsts, new_seconds = refs[27:35], refs[35:43], refs[43:51]
    norm_ref, rms_ref = refs[51:53]
    for index in range(3):
        refs[53 + index][...] = passed[index][...]
    width = params[0].shape[2]
    heads, known = params[7].shape
    gains = sums[0:3, :]
    by_head = jnp.concatenate(
        [sums[8 : 8 + heads // 2, 0:128], sums[16 : 16 + heads // 2, 0:128]], axis=0
    )[:, :known]
    whole = lambda value: jnp.sum(jnp.sum(value, axis=1, keepdims=True), axis=0, keepdims=True)
    norm = jnp.sqrt(whole(squares[...]) + whole(gains * gains) + whole(by_head * by_head))
    factor = jnp.minimum(1.0, clip_limit / (norm + 1e-06))
    norm_ref[...] = norm
    counted = sums[5:6, 0:1] * D
    rms_ref[...] = jnp.concatenate(
        [jnp.sqrt(whole(sums[3:4, :]) / counted), jnp.sqrt(whole(sums[4:5, :]) / counted)], axis=1
    )

    def update(index, at, grad):
        decay = weight_decay if index < 6 else 0.0
        weight, moment, second = adamw(
            params[index][at], firsts[index][at], seconds[index][at], grad * factor, decay,
            learn_rates[index],
        )
        news[index][at] = weight
        new_firsts[index][at] = moment
        new_seconds[index][at] = second

    columns = lambda piece, start, count: grads[piece, :, pl.ds(start, count)]
    for index, base in ((0, 0), (2, 2)):
        update(index, (0,), columns(base, 0, width))
        update(index, (1,), columns(base, width, width))
        update(index, (2,), columns(base + 1, 0, width))
        update(index + 1, (slice(None),), columns(base + 1, width, width))
    for tile in range(params[5].shape[1] // FEED_TILE):
        at = pl.ds(tile * FEED_TILE, FEED_TILE)
        for part in range(2):
            update(4, (part, slice(None), at), columns(4 + tile, part * FEED_TILE, FEED_TILE))
        update(5, (slice(None), at), columns(4 + tile, 2 * FEED_TILE, FEED_TILE))
    update(6, (slice(None),), gains)
    update(7, (slice(None),), by_head)


TURNED = (1, 3, 5, 7)


def turned_views(group):
    return [member.T if index in TURNED else member for index, member in enumerate(group)]


def adam(grads, sums, squares, params, firsts, seconds, passed):
    params, firsts, seconds = (turned_views(group) for group in (params, firsts, seconds))
    same = [jax.ShapeDtypeStruct(member.shape, F32) for member in params]
    outs = same * 3 + [jax.ShapeDtypeStruct((1, 1), F32), jax.ShapeDtypeStruct((1, 2), F32)]
    outs += [jax.ShapeDtypeStruct(member.shape, member.dtype) for member in passed]
    made = pl.pallas_call(
        adam_kernel,
        out_shape=tuple(outs),
        in_specs=[VMEM] * 30,
        out_specs=(VMEM,) * 29,
        compiler_params=pltpu.CompilerParams(vmem_limit_bytes=60 * 2**20),
    )(grads, sums, squares, *params, *firsts, *seconds, *passed)
    groups = [turned_views(made[start : start + 8]) for start in (0, 8, 16)]
    return (sum(groups, []), made[24], made[25], made[26:])


def fused(*args):
    (decoder_in, encoder_out, out_grad, block_items, block_lengths, target_lengths) = args[:6]
    params, firsts, seconds = args[6:14], args[14:22], args[22:30]
    norm_gains, position_bias = params[6:]
    blocks = lax.axis_size("blk")
    length = 2 * decoder_in.shape[0]
    key_rows = encoder_out.shape[0]
    width = params[0].shape[2]
    rows = params[0].shape[1]
    per_chip = key_rows // KB
    total_blocks = blocks * per_chip
    most = total_blocks - blocks * target_lengths.shape[0] + 1
    slots = -(-most // 6) * 6
    tiles = length // 128
    offsets = np.arange(256)
    steps = np.where(offsets < 128, offsets, offsets - 256)[None] + 128 * np.arange(tiles)[:, None]
    one_hot = np.eye(position_bias.shape[0], dtype=np.float32)[bucket_of(np.maximum(steps, 0))]
    one_hot = one_hot * (steps >= 0)[..., None]
    buckets = np.zeros((tiles, 256, 128), np.float32)
    buckets[:, :, : one_hot.shape[2]] = one_hot
    blank = np.where(steps >= 0, 0.0, masked_score).astype(np.float32).reshape(1, -1)
    shapes = front_shapes(blocks, slots, length, width, rows, 8 * width // PIECE)
    weights = turned_views(params)[:6]
    operands = weights + [
        encoder_out, decoder_in, out_grad, norm_gains, position_bias.T,
        jnp.asarray(one_hot.reshape(tiles * 256, -1).T), jnp.asarray(blank),
    ]
    scalars = [block_items, block_lengths, target_lengths]
    made = front(blocks, slots, shapes, operands, scalars, per_chip)
    grads, decoder_grad, encoder_grad, sums, squares = back(
        blocks, slots, shapes, made, decoder_in, norm_gains, target_lengths,
        jnp.asarray(buckets, BF), key_rows,
    )
    layer_out = made[FRONT_OUT.index("layer_out")]
    updated, norm, rms, passed = adam(
        grads, sums, squares, params, firsts, seconds, [layer_out, decoder_grad, encoder_grad]
    )
    return (*passed, *updated, norm.reshape(()), rms.reshape(2))


def plain_body(
    decoder_in,
    encoder_out,
    out_grad,
    block_items,
    block_lengths,
    target_lengths,
    self_proj,
    self_out,
    cross_proj,
    cross_out,
    feed_in,
    feed_out,
    norm_gains,
    position_bias,
    *moments,
):
    core = lax.axis_index("mp")
    rank = lax.axis_index("blk")
    blocks = lax.axis_size("blk")
    rows_own = decoder_in.shape[0]
    length = 2 * rows_own
    half = self_proj.shape[2]
    heads = half // DH
    hidden_half = feed_in.shape[2]
    key_rows = encoder_out.shape[0]

    params = [self_proj, self_out, cross_proj, cross_out, feed_in, feed_out]
    flat = []
    for value in params:
        if value.ndim == 3:
            flat.extend(value[index].astype(BF) for index in range(value.shape[0]))
        else:
            flat.append(value.astype(BF).T)
    shard = jnp.concatenate(flat, axis=1)
    edges = np.cumsum([0] + [member.shape[1] for member in flat]).tolist()
    places = jnp.arange(key_rows, dtype=jnp.int32)
    tags_own = jnp.where(
        places % KB < jnp.repeat(block_lengths, KB), jnp.repeat(block_items, KB), -1
    )
    encoder_half = lax.dynamic_slice_in_dim(encoder_out, core * (D // 2), D // 2, 1)
    weights = lax.all_gather(shard, "blk", axis=0, tiled=True)
    encoder = lax.all_gather(encoder_out, "blk", axis=0, tiled=True)
    tags = lax.all_gather(tags_own, "blk", axis=0, tiled=True)
    tokens = lax.all_gather(decoder_in, "mp")
    upstream = lax.all_gather(out_grad, "mp")
    tokens = tokens.reshape(length, D).astype(F32)
    limit = target_lengths[0]
    valid = (jnp.arange(length, dtype=jnp.int32) < limit).astype(F32)[:, None]
    dy = upstream.reshape(length, D).astype(F32) * valid
    w_q, w_k, w_v, w_so, c_q, c_k, c_v, w_co, f_g, f_u, f_d = (
        weights[:, edges[index] : edges[index + 1]] for index in range(11)
    )

    def both(term):
        pair = lax.all_gather(term, "mp")
        return pair[0] + pair[1]

    def dot(left, right, dims=((1,), (0,))):
        return lax.dot_general(left, right, (dims, ((), ())), preferred_element_type=F32)

    NT = ((1,), (1,))
    TN = ((0,), (0,))
    h1 = rms_norm(tokens, norm_gains[0]).astype(BF)
    q1, k1, v1 = (dot(h1, w).astype(BF).reshape(length, heads, DH) for w in (w_q, w_k, w_v))
    bias_here = lax.dynamic_slice_in_dim(position_bias, core * heads, heads, 1)
    spots = np.arange(length)
    buckets = bucket_of(np.maximum(spots, 0))
    by_distance = jnp.dot(
        jnp.asarray(np.eye(position_bias.shape[0], dtype=np.float32)[buckets]),
        bias_here,
        precision=HIGHEST,
    )
    tiles = length // 128
    offsets = np.arange(256)
    steps = np.where(offsets < 128, -offsets, 256 - offsets)[None] + 128 * np.arange(tiles)[:, None]
    strips = jnp.where(
        steps[None] >= 0, by_distance.T[:, np.maximum(np.minimum(steps, length - 1), 0)], masked_score
    )
    diagonals = pl.pallas_call(
        toeplitz_kernel,
        out_shape=jax.ShapeDtypeStruct((heads * tiles, 128, 128), F32),
        in_specs=[VMEM],
        out_specs=VMEM,
    )(strips.reshape(heads * tiles, 1, 256)).reshape(heads, tiles, 128, 128)
    blank = jnp.full((heads, 128, 128), masked_score)
    bias = jnp.concatenate(
        [
            jnp.concatenate([diagonals[:, i - j] if i >= j else blank for j in range(tiles)], 2)
            for i in range(tiles)
        ],
        1,
    )
    s1 = jnp.einsum("qhd,khd->hqk", q1, k1, preferred_element_type=F32) + bias
    p1 = jnp.exp(s1 - jnp.max(s1, -1, keepdims=True))
    p1 = p1 / jnp.sum(p1, -1, keepdims=True)
    p1_low = p1.astype(BF)
    o1 = jnp.einsum("hqk,khd->qhd", p1_low, v1, preferred_element_type=F32).astype(BF)
    o1 = o1.reshape(length, half)
    x1 = tokens + both(dot(o1, w_so, NT))
    h2 = rms_norm(x1, norm_gains[1]).astype(BF)
    q2 = dot(h2, c_q).astype(BF).reshape(length, heads, DH)
    total_blocks = tags.shape[0] // KB
    items = blocks * target_lengths.shape[0]
    most = total_blocks - items + 1
    owned = tags.reshape(total_blocks, KB)[:, 0] == rank
    order = jnp.argsort(jnp.logical_not(owned), stable=True)[:most]
    enc = encoder.reshape(total_blocks, KB, D)[order].reshape(most * KB, D)
    mine = (tags.reshape(total_blocks, KB)[order].reshape(most * KB) == rank)
    kc = dot(enc, c_k).astype(BF).reshape(-1, heads, DH)
    vc = dot(enc, c_v).astype(BF).reshape(-1, heads, DH)

    def cross_forward(parts):
        q, k, v = parts
        s = jnp.where(mine[None], dot(q, k, NT), masked_score)
        top = jnp.max(s, -1, keepdims=True)
        e = jnp.exp(s - top)
        total = jnp.sum(e, -1, keepdims=True)
        return (dot((e / total).astype(BF), v).astype(BF), top + jnp.log(total))

    by_head = lambda value: jnp.swapaxes(value.reshape(value.shape[0], heads, DH), 0, 1)
    q2h, kch, vch = by_head(q2), by_head(kc), by_head(vc)
    o2, lse = lax.map(cross_forward, (q2h, kch, vch))
    o2 = jnp.swapaxes(o2, 0, 1).reshape(length, half)
    x2 = x1 + both(dot(o2, w_co, NT))
    h3 = rms_norm(x2, norm_gains[2]).astype(BF)
    gate, upper = dot(h3, f_g), dot(h3, f_u)
    hidden_full, pull = jax.vjp(lambda g, u: jax.nn.gelu(g, approximate=True) * u, gate, upper)
    hidden = hidden_full.astype(BF)
    y = x2 + both(dot(hidden, f_d, NT))
    df = dy.astype(BF)
    g_fd = dot(df, hidden, TN)
    dgate, dup = (member.astype(BF) for member in pull(dot(df, f_d)))
    g_fg, g_fu = dot(h3, dgate, TN), dot(h3, dup, TN)
    dn3 = both(dot(dgate, f_g, NT) + dot(dup, f_u, NT))
    delta, gain3 = norm_back(x2, norm_gains[2], dn3)
    dx2 = dy + delta
    da2 = dx2.astype(BF)
    g_co = dot(da2, o2, TN)
    do2 = dot(da2, w_co).astype(BF)

    def cross_backward(parts):
        q, k, v, do, total = parts
        s = jnp.where(mine[None], dot(q, k, NT), masked_score)
        p = jnp.exp(s - total)
        dp = dot(do, v, NT)
        ds = (p * (dp - jnp.sum(p * dp, -1, keepdims=True))).astype(BF)
        return (
            dot(ds, k).astype(BF), dot(ds, q, TN).astype(BF), dot(p.astype(BF), do, TN).astype(BF)
        )

    dq2, dkc, dvc = lax.map(cross_backward, (q2h, kch, vch, by_head(do2), lse))
    flat_heads = lambda value: jnp.swapaxes(value, 0, 1).reshape(-1, half)
    dq2, dkc, dvc = flat_heads(dq2), flat_heads(dkc), flat_heads(dvc)
    g_cq, g_ck, g_cv = dot(h2, dq2, TN), dot(enc, dkc, TN), dot(enc, dvc, TN)
    enc_term = dot(dkc, c_k, NT) + dot(dvc, c_v, NT)
    spread = jnp.zeros((total_blocks, KB, D), BF).at[order].set(
        enc_term.astype(BF).reshape(most, KB, D)
    )
    encoder_grad = lax.psum_scatter(
        lax.psum_scatter(spread.reshape(-1, D), "mp", scatter_dimension=1, tiled=True),
        "blk", scatter_dimension=0, tiled=True,
    ).astype(F32)
    dn2 = both(dot(dq2, c_q, NT))
    delta, gain2 = norm_back(x1, norm_gains[1], dn2)
    dx1 = dx2 + delta
    da1 = dx1.astype(BF)
    g_so = dot(da1, o1, TN)
    do1 = dot(da1, w_so).astype(BF).reshape(length, heads, DH)
    dp1 = jnp.einsum("qhd,khd->hqk", do1, v1, preferred_element_type=F32)
    ds1 = (p1 * (dp1 - jnp.sum(p1 * dp1, -1, keepdims=True))).astype(BF)
    ds_wide = ds1.astype(F32)
    bucket_grid = jnp.asarray(bucket_of(np.maximum(spots[:, None] - spots[None, :], 0)).astype(np.int32))
    bias_sums = lax.map(
        lambda b: jnp.sum(jnp.where(bucket_grid[None] == b, ds_wide, 0.0), axis=(1, 2)),
        jnp.arange(position_bias.shape[0], dtype=jnp.int32),
    )
    grad_bias = lax.dynamic_update_slice_in_dim(
        jnp.zeros(position_bias.shape, F32), bias_sums, core * heads, 1
    )
    dq1 = jnp.einsum("hqk,khd->qhd", ds1, k1, preferred_element_type=F32)
    dk1 = jnp.einsum("hqk,qhd->khd", ds1, q1, preferred_element_type=F32)
    dv1 = jnp.einsum("hqk,qhd->khd", p1_low, do1, preferred_element_type=F32)
    dq1, dk1, dv1 = (member.astype(BF).reshape(length, half) for member in (dq1, dk1, dv1))
    g_q, g_k, g_v = dot(h1, dq1, TN), dot(h1, dk1, TN), dot(h1, dv1, TN)
    dn1 = both(dot(dq1, w_q, NT) + dot(dk1, w_k, NT) + dot(dv1, w_v, NT))
    delta, gain1 = norm_back(tokens, norm_gains[0], dn1)
    decoder_grad = dx1 + delta
    grads = jnp.concatenate(
        [member.astype(BF) for member in (g_q, g_k, g_v, g_so, g_cq, g_ck, g_cv, g_co, g_fg, g_fu, g_fd)],
        axis=1,
    )
    mine_grad = lax.psum_scatter(grads.astype(F32), "blk", scatter_dimension=0, tiled=True)
    pieces = [mine_grad[:, edges[index] : edges[index + 1]] for index in range(11)]
    shards = (
        jnp.stack(pieces[0:3]), pieces[3].T, jnp.stack(pieces[4:7]), pieces[7].T,
        jnp.stack(pieces[8:10]), pieces[10].T,
    )
    square_sum = jnp.sum(mine_grad * mine_grad)
    stat_terms = jnp.stack(
        [jnp.sum(valid * y * y), jnp.sum(valid * decoder_grad * decoder_grad), jnp.sum(valid)]
    )
    gain_grads, bias_grads, square_total, stat_total = lax.psum(
        (jnp.stack([gain1, gain2, gain3]) * 0.5, grad_bias, square_sum, stat_terms), ("blk", "mp")
    )
    grad_norm = jnp.sqrt(
        square_total + jnp.sum(gain_grads * gain_grads) + jnp.sum(bias_grads * bias_grads)
    )
    factor = jnp.minimum(1.0, clip_limit / (grad_norm + 1e-06))
    params = params + [norm_gains, position_bias]
    gradients = shards + (gain_grads, bias_grads)
    updated = [
        adamw(
            params[index], moments[index], moments[8 + index], gradients[index] * factor,
            weight_decay if index < 6 else 0.0, learn_rates[index],
        )
        for index in range(8)
    ]
    token_rms = jnp.sqrt(stat_total[:2] / (stat_total[2] * D))
    own = lambda value: lax.dynamic_slice_in_dim(value, core * rows_own, rows_own, 0)
    return (
        own(y).astype(BF),
        own(decoder_grad),
        encoder_grad,
        *(entry[0] for entry in updated),
        *(entry[1] for entry in updated),
        *(entry[2] for entry in updated),
        grad_norm,
        token_rms,
    )


def solution(mesh):
    proj, out = P(None, "blk", "mp"), P("mp", "blk")
    family = (proj, out, proj, out, proj, out, P(), P())
    tokens = P(("blk", "mp"), None)
    tiled = mesh.shape["blk"] == 16 and D // mesh.shape["blk"] % 16 == 0
    return jax.shard_map(
        fused if tiled else plain_body,
        mesh=mesh,
        in_specs=(tokens, P("blk", None), tokens, P("blk"), P("blk"), P("blk")) + family * 3,
        out_specs=(tokens, tokens, P("blk", "mp")) + family * 3 + (P(), P()),
        check_vma=False,
    )
```

time: 1660 us -> 279 us (0.17)
  waiting for transfers between devices: 1050 us -> 0 us
  Pallas kernels: 0 us -> 271 us
  matrix products: 190 us -> 0 us
  blocking collectives: 181 us -> 0 us
  other arithmetic: 106 us -> 0 us
  local copies, waits for them, and re-layouts: 94.7 us -> 0 us
  between operations: 24.7 us -> 1.8 us
    reduce_scatter x10 -> x0, waiting for transfers between devices: 463 us -> none  [the longest x1 127 us: body(): lax.psum_scatter(grad_sout, 'blk', scatter_dimension=1, tiled=True)]
    unnamed x20 -> x0, waiting for transfers between devices: 444 us -> none
    pallas_call x0 -> x3, Pallas kernels: none -> 271 us  [the longest x1 140 us: back(): pl.pallas_call(functools.partial(back_kernel, levels, slots), out_shape=o...]
    dot_general x37 -> x0, matrix products: 190 us -> none  [the longest x1 21.8 us: inner(): jnp.einsum('hqk,khd->hqd', weights_now, value_rows, precision=HIGHEST)]
    all_gather x6 -> x0, waiting for transfers between devices: 146 us -> none  [the longest x1 68.7 us: body(): lax.all_gather(feed_in.astype(jnp.bfloat16), 'blk', axis=1, tiled=True)]
    all_gather x9 -> x0, blocking collectives: 141 us -> none  [the longest x1 47.5 us: body(): lax.all_gather(self_out.astype(jnp.bfloat16), 'blk', axis=1, tiled=True)]
    eq x1 -> x0, local copies, waits for them, and re-layouts: 46.3 us -> none  [body(): buckets[:, :, None]]
    psum x1 -> x0, blocking collectives: 40 us -> none  [body(): lax.psum((jnp.stack([gain_one, gain_two, gain_three]), grad_bias, square_...]
  transfers between devices with their start and end apart: 18 -> 0, of which waited for: 13 -> 0; matrix products, arithmetic and copies ran while one was open for 17% -> 0% of each run, Pallas kernels for 0% -> 0%
where the time goes in v1:
time: 279 us; the launch traced here: 273 us
  Pallas kernels  271 us (97%)
    pallas_call x1, Pallas kernels, back(): pl.pallas_call(functools.partial(back_kernel, levels, slots), out_shape=o...  140 us
    pallas_call x1, Pallas kernels, front(): pl.pallas_call(functools.partial(front_kernel, levels, slots), out_shape=...  125 us
    pallas_call x1, Pallas kernels, adam(): pl.pallas_call(adam_kernel, out_shape=tuple(outs), in_specs=[VMEM] * 30,...  5.58 us

profile of v1, /device:TPU:0, one launch (start us, length us, event | category | flops | bytes accessed | tf_op | source)
XLA Modules:
  0.0 273.2 jit_solution(6875733555777729787)
XLA Ops:
  1.3 125.4 %shard_map.536 = (bf16[4,4,4,48,768]{4,3,2,1,0:T(8,128)(2,1)}, f32[24,128,128]{2,1,0:T(8,128)}, bf16[512,768]{1,0:T(8,128)(2,1)}, bf16[512,1152]{1,0:T(8,128)(2,...) custom-call(f32[3,48,384]{2,1,0:T(8,128)} %refs_0_.1, ...), custom_call_target="tpu_custom_call" | custom-call | tf_op jit(solution)/shard_map/pallas_call | solution.py:1030
  126.7 140.5 %shard_map.537 = (f32[8,48,768]{2,1,0:T(8,128)}, f32[256,768]{1,0:T(8,128)}, f32[128,384]{1,0:T(8,128)}, f32[24,768]{1,0:T(8,128)}, f32[8,128]{1,0:T(8,128)}) custom-call(f32[3,768]{1,0:T(4,128)} %refs_6_.1, bf16[256,768]{1,0:T(8,128)(2,1)} %tok_own.3, bf16[4,256,128]{2,1,0:T(8,128)(2,1)} %constant.8.clone.buckets, s32[32]{0:T(128)} %get-tuple-element.85.slot_of, ...), custom_call_target="tpu_custom_call" | custom-call | tf_op jit(solution)/shard_map/pallas_call | solution.py:1315
  267.2 5.6 %shard_map.538 = (f32[3,48,384]{2,1,0:T(8,128)}, f32[48,384]{1,0:T(8,128)}, f32[3,48,384]{2,1,0:T(8,128)}, f32[48,384]{1,0:T(8,128)}, f32[2,48,1024]{2,1,0:T(8,1...) custom-call(f32[8,48,768]{2,1,0:T(8,128)} %get-tuple-element.106.gra, ...), custom_call_target="tpu_custom_call" | custom-call | tf_op jit(solution)/shard_map/pallas_call | solution.py:1395
